TPU v7x, 256 devices: a whole 4x4x8 slice. The times are simulated.
256 devices in a mesh: row: 64 (over z, x, core), col: 4 (over y).
Axes of the slice: x: 4, y: 4, z: 8, core: 2. Of those that a mesh axis runs over, the one named last changes fastest.
Arguments:
- rhs: float32 [512, 72, 64], P('row', None, 'col'), may hold values from -60 to 60
- system_lower: float32 [512, 8, 72, 72], P('row', 'col'), may hold values from -0.625 to 0.625
- system_diag: float32 [512, 72, 72], P('row'), may hold values from -16 to 20, as said below
- factor_lower: float32 [512, 8, 72, 72], P('row'), may hold values from -0.4375 to 0.4375
- diag_inverse: float32 [512, 72, 72], P('row'), may hold values from -0.25 to 2, as said below
- neighbours: int32 [512, 8], P('row'), may hold values from -1 to 510, as said below
- counts: int32 [512], P('row'), may hold values from 0 to 8, as said below
Outputs:
- solution: float32 [512, 72, 64], P('row', None, 'col')
- residual: float32 [512, 72, 64], P('row', None, 'col')
- direction: float32 [512, 72, 64], P('row', None, 'col')
Inputs may be any that keep to these rules, and one draw needn't show every extreme that they name: `neighbours`: block rows come in aligned groups of 8. Entries k < counts[i] of row i name distinct block rows j < i that lie in the group of i or are the last two block rows of the group before; entry 0 is i - 1 for every i >= 1; all other entries are -1. `counts`: block row 0 has no neighbours, every other block row at least one, and the last block row of every group but the first has 8. `diag_inverse`: each block is lower triangular with its diagonal entries between 0.5 and 2. `system_diag`: each block is symmetric positive definite.
All inputs are finite; a program needn't handle non-finite values.
Results may differ from a plain program's by a relative error of at most 0.0003.
Values sent between devices are 32-bit elements; how exact they have to be, the bound alone decides.
A program may use at most 64 MiB of HBM per device.

v0:
```python
import jax
import jax.numpy as jnp
from jax import lax
from jax.sharding import PartitionSpec as P

ITERS = 2


HIGH = lax.Precision.HIGHEST


def carried_in(x, axis, combine, identity, reverse):
    count, here = (lax.axis_size(axis), lax.axis_index(axis))
    everything = jax.tree.map(lambda part: lax.all_gather(part, axis), x)
    start = jax.tree.map(
        lambda part, zero: jnp.broadcast_to(jnp.asarray(zero, part.dtype), part.shape), x, identity
    )

    def turn(k, before):
        at = count - 1 - k if reverse else k
        reached = at > here if reverse else at < here
        new = combine(before, jax.tree.map(lambda part: part[at], everything))
        return jax.tree.map(lambda a, b: jnp.where(reached, a, b), new, before)

    return lax.fori_loop(0, count, turn, start)


def shifted(value, axis, steps):
    count = lax.axis_size(axis)
    first, last = (max(0, -steps), min(count, count - steps))
    return lax.ppermute(value, axis, [(source, source + steps) for source in range(first, last)])


def compose(earlier, later):
    return (
        jnp.dot(later[0], earlier[0], precision=HIGH),
        jnp.dot(later[0], earlier[1], precision=HIGH) + later[1],
    )


def forward_local(factor_lower, diag_inverse, local_slots, live, source, incoming):
    rows = source.shape[0]
    start_buffer = jnp.concatenate([incoming, jnp.zeros_like(source)], axis=0)

    def advance(row, buffer):
        picked = buffer[local_slots[row]] * live[row][:, None, None]
        gathered_sum = jnp.einsum("kab,kbc->ac", factor_lower[row], picked, precision=HIGH)
        value = jnp.dot(diag_inverse[row], source[row] - gathered_sum, precision=HIGH)
        return lax.dynamic_update_index_in_dim(buffer, value, row + 2, 0)

    return lax.fori_loop(0, rows, advance, start_buffer)


def backward_local(factor_lower, diag_inverse, local_slots, live, source, incoming):
    rows = source.shape[0]
    carry_start = jnp.concatenate([jnp.zeros_like(source), incoming], axis=0)

    def retreat(turn, state):
        carried, solved = state
        row = rows - 1 - turn
        value = jnp.dot(diag_inverse[row].T, source[row] - carried[row + 2], precision=HIGH)
        shares = (
            jnp.einsum("kab,ac->kbc", factor_lower[row], value, precision=HIGH)
            * live[row][:, None, None]
        )
        carried = carried.at[local_slots[row]].add(shares)
        solved = lax.dynamic_update_index_in_dim(solved, value, row, 0)
        return (carried, solved)

    carried, solved = lax.fori_loop(0, rows, retreat, (carry_start, jnp.zeros_like(source)))
    return (solved, carried[:2])


def precondition(factor_lower, diag_inverse, local_slots, live, residual):
    rows, width, columns = residual.shape
    span = 2 * width
    unit = jnp.eye(span, dtype=jnp.float32).reshape(2, width, span)
    pad_rows = jnp.zeros((rows, width, span), jnp.float32)
    zero_rim = jnp.zeros((2, width, columns), jnp.float32)
    incoming = jnp.concatenate([zero_rim, unit], axis=2)
    identity = (jnp.eye(span, dtype=jnp.float32), jnp.zeros((span, columns), jnp.float32))
    source = jnp.concatenate([residual, pad_rows], axis=2)
    buffer = forward_local(factor_lower, diag_inverse, local_slots, live, source, incoming)
    rim = buffer[rows:].reshape(span, columns + span)
    _, entering = carried_in((rim[:, columns:], rim[:, :columns]), "row", compose, identity, False)
    solved = forward_local(
        factor_lower, diag_inverse, local_slots, live, residual, entering.reshape(2, width, columns)
    )[2:]
    source = jnp.concatenate([solved, pad_rows], axis=2)
    values, leaving = backward_local(
        factor_lower, diag_inverse, local_slots, live, source, incoming
    )
    rim = leaving.reshape(span, columns + span)
    _, entering = carried_in((rim[:, columns:], rim[:, :columns]), "row", compose, identity, True)
    return backward_local(
        factor_lower, diag_inverse, local_slots, live, solved, entering.reshape(2, width, columns)
    )[0]


def upper_part(blocks, slots, live, vector):
    rows = vector.shape[0]
    shares = jnp.einsum("rkab,rac->rkbc", blocks, vector, precision=HIGH)
    target = (slots[:, :, None] == jnp.arange(rows + 2, dtype=jnp.int32)[None, None, :]).astype(
        jnp.float32
    )
    target = target * live[:, :, None]
    return jnp.einsum("rks,rkbc->sbc", target, shares, precision=HIGH)


def combine_upper(partial_value):
    rows = partial_value.shape[0] - 2
    coming = shifted(partial_value[:2], "row", -1)
    return partial_value[2:].at[rows - 2 :].add(coming)


def finish_lower(blocks, slots, live, inner):
    rows = inner.shape[0]
    rim = shifted(inner[rows - 2 :], "row", 1)
    extended = jnp.concatenate([rim, inner], axis=0)
    picked = extended[slots] * live[:, :, None, None]
    return jnp.einsum("rkab,rkbc->rac", blocks, picked, precision=HIGH)


def system_times(blocks, system_diag, local_slots, live, direction):
    rows, width, columns = direction.shape
    diagonal_part = jnp.einsum("rab,rbc->rac", system_diag, direction, precision=HIGH)
    share = blocks.shape[1]
    first = lax.axis_index("col") * share
    part_slots = lax.dynamic_slice_in_dim(local_slots, first, share, 1)
    part_live = lax.dynamic_slice_in_dim(live, first, share, 1)
    every = lax.all_gather(direction, "col", axis=2, tiled=True)
    partial_value = combine_upper(upper_part(blocks, part_slots, part_live, every))
    inner = lax.psum(partial_value, "col") + every
    terms = finish_lower(blocks, part_slots, part_live, inner)
    own = lax.psum_scatter(terms, "col", scatter_dimension=2, tiled=True)
    inner_own = lax.dynamic_slice_in_dim(inner, lax.axis_index("col") * columns, columns, 2)
    return own + inner_own + diagonal_part


def global_dot(left, right):
    return lax.psum(jnp.sum(left * right, axis=(0, 1)), "row")


def per_device(rhs, system_lower, system_diag, factor_lower, diag_inverse, neighbours, counts):
    rows = rhs.shape[0]
    local_slots = jnp.clip(neighbours - lax.axis_index("row") * rows + 2, 0, rows + 1)
    live = (jnp.arange(neighbours.shape[1], dtype=jnp.int32)[None, :] < counts[:, None]).astype(
        jnp.float32
    )
    solution = jnp.zeros_like(rhs)
    residual = rhs
    precond = precondition(factor_lower, diag_inverse, local_slots, live, residual)
    direction = precond
    energy = global_dot(residual, precond)
    for step in range(ITERS):
        image = system_times(system_lower, system_diag, local_slots, live, direction)
        alpha = energy / lax.psum(jnp.sum(direction * image, axis=(0, 1)), "row")
        solution = solution + alpha * direction
        residual = residual - alpha * image
        precond = precondition(factor_lower, diag_inverse, local_slots, live, residual)
        energy_next = global_dot(residual, precond)
        direction = precond + energy_next / energy * direction
        energy = energy_next
    return (solution, residual, direction)


def solution(mesh):
    in_specs = (
        P("row", None, "col"),
        P("row", "col", None, None),
        P("row", None, None),
        P("row", None, None, None),
        P("row", None, None),
        P("row", None),
        P("row"),
    )
    out_specs = (P("row", None, "col"), P("row", None, "col"), P("row", None, "col"))
    return jax.shard_map(
        per_device, mesh=mesh, in_specs=in_specs, out_specs=out_specs, check_vma=False
    )
```

profile of v0, /device:TPU:1, one launch (start us, length us, event | category | flops | bytes accessed | tf_op | source)
XLA Modules:
  0.0 2151.6 jit_solution(15287763720875697901)
XLA Ops:
  12.7 50.3 %while.290 = (s32[]{:T(128)}, f32[10,72,160]{2,1,0:T(8,128)}, f32[8,72,72]{2,1,0:T(8,128)}, f32[8,72,160]{2,1,0:T(8,128)}, f32[8,8,72,72]{3,2,1,0:T(8,128)S(1)},...) while((s32[]{:T(128)}, f32[10,72,160]{2,1,0:T(8,128)}, ...), condition=%wide.region_1.2_spmd, body=%wide.region_0.1_spmd.sunk | while | flops 89684256 | bytes 1932647 | solution.py:51
  68.9 59.3 %all-gather.12 = f32[64,144,16]{1,2,0:T(8,128)} all-gather(f32[1,144,16]{1,2,0:T(8,128)S(1)} %copy.112), channel_id=3, replica_groups=mesh['row'=64,'col'=4] {'row'}, dimensions={0}, use_global_device_ids=true | all-gather | bytes 599040 | tf_op jit(solution)/shard_map/all_gather | solution.py:14
  128.2 26.0 %all-gather.25.cloned.1.call-done = f32[9216,144]{1,0:T(8,128)} async-done(((f32[144,144]{1,0:T(8,128)}), f32[9216,144]{1,0:T(8,128)}) %all-gather.25.cloned.1.call-update) | async-done | bytes 5308432 | tf_op jit(solution)/shard_map/all_gather | solution.py:14
  154.1 77.0 %while.302 = (s32[]{:T(128)}, f32[144,16]{0,1:T(8,128)S(1)}, s32[]{:T(128)}, f32[64,144,144]{2,1,0:T(8,128)}, f32[64,144,16]{1,2,0:T(8,128)}, /*index=5*/s32[]{:T(128)}, s32[]{:T(128)}) while((s32[]{:T(128)}, f32[144,16]{0,1:T(8,128)S(1)}, s32[]{:T(128)}, f32[64,144,144]{2,1,0:T(8,128)}, f32[64,144,16]{1,2,0:T(8,128)}, ...), condition=%wide.region_3.4_spmd.clone, body=%wide.region_2.3_spmd.clone.sunk | while | flops 3990532 | bytes 226911 | solution.py:25
  231.2 26.6 %while.291 = (s32[]{:T(128)}, f32[10,72,16]{1,2,0:T(8,128)S(1)}, f32[8,72,72]{2,1,0:T(8,128)}, f32[8,72,16]{1,2,0:T(8,128)}, f32[8,8,72,72]{3,2,1,0:T(8,128)S(1)...) while((s32[]{:T(128)}, f32[10,72,16]{1,2,0:T(8,128)S(1)}, ...), condition=%wide.region_5.6_spmd, body=%wide.region_4.5_spmd.sunk | while | flops 8969374 | bytes 506727 | solution.py:51
  258.9 51.1 %while.292 = (s32[]{:T(128)}, f32[10,72,160]{2,1,0:T(8,128)}, s32[8,8]{1,0:T(8,128)S(1)}, f32[8,8,72,72]{2,3,1,0:T(8,128)}, f32[8,72,72]{2,1,0:T(8,128)}, /*inde...) while((s32[]{:T(128)}, f32[10,72,160]{2,1,0:T(8,128)}, ...), condition=%wide.region_8.9_spmd, body=%wide.region_6.8_spmd.sunk | while | flops 89775392 | bytes 2047909 | solution.py:70
  268.7 3.0 scatter_fusion
  312.8 53.7 %all-gather.13 = f32[64,144,16]{1,2,0:T(8,128)} all-gather(f32[1,144,16]{1,2,0:T(8,128)S(1)} %copy.118), channel_id=5, replica_groups=mesh['row'=64,'col'=4] {'row'}, dimensions={0}, use_global_device_ids=true | all-gather | bytes 599040 | tf_op jit(solution)/shard_map/all_gather | solution.py:14
  366.5 27.2 %all-gather.27.cloned.1.call-done = f32[9216,144]{1,0:T(8,128)} async-done(((f32[144,144]{1,0:T(8,128)}), f32[9216,144]{1,0:T(8,128)}) %all-gather.27.cloned.1.call-update) | async-done | bytes 5308432 | tf_op jit(solution)/shard_map/all_gather | solution.py:14
  393.7 77.4 %while.303 = (s32[]{:T(128)}, f32[144,16]{0,1:T(8,128)S(1)}, s32[]{:T(128)}, f32[64,144,144]{2,1,0:T(8,128)}, f32[64,144,16]{1,2,0:T(8,128)}, /*index=5*/s32[]{:T(128)}, s32[]{:T(128)}, s32[]{:T(128)}, s32[]{:T(128)}) while((s32[]{:T(128)}, f32[144,16]{0,1:T(8,128)S(1)}, s32[]{:T(128)}, f32[64,144,144]{2,1,0:T(8,128)}, ...), condition=%wide.region_10.11_spmd.clone, body=%wide.region_9.10_spmd.clone.sunk | while | flops 3990536 | bytes 226973 | solution.py:25
  471.2 22.0 %while.293 = (s32[]{:T(128)}, f32[10,72,16]{1,2,0:T(8,128)S(1)}, f32[8,72,16]{1,2,0:T(8,128)S(1)}, s32[8,8]{1,0:T(8,128)S(1)}, f32[8,8,72,72]{3,2,1,0:T(8,128)S(...) while((s32[]{:T(128)}, f32[10,72,16]{1,2,0:T(8,128)S(1)}, ...), condition=%wide.region_13.14_spmd, body=%wide.region_11.13_spmd.sunk | while | flops 8977570 | bytes 523149 | solution.py:70
  493.2 10.3 all_gather.86
  505.2 4.4 collective-permute-start
  512.2 43.0 %all-reduce.19.cloned.1.call-done = f32[8,72,64]{1,0,2:T(8,128)} async-done(((f32[8,72,64]{1,0,2:T(8,128)}), f32[8,72,64]{1,0,2:T(8,128)}) %all-reduce.19.cloned.1.call-update) | async-done | bytes 147472 | tf_op jit(solution)/shard_map/psum | solution.py:133
  556.9 6.0 collective-permute-start.1
  571.0 21.4 reduce-scatter.3.cloned.1.call-done
  593.4 126.8 %all-reduce.15 = (f32[16]{0:T(128)S(1)}, f32[16]{0:T(128)S(1)}) all-reduce(f32[16]{0:T(128)S(1)} %multiply_reduce_fusion.4, f32[16]{0:T(128)S(1)} %get-tuple-element.3802), channel_id=1, replica_groups=mesh['row'=64,'col'=4] {'row'}, use_global_device_ids=true, to_apply=%region_15.16 | all-reduce | flops 32 | bytes 256 | tf_op jit(solution)/shard_map/psum | solution.py:141
  722.3 50.3 %while.294 = (s32[]{:T(128)}, f32[10,72,160]{2,1,0:T(8,128)}, f32[8,72,72]{2,1,0:T(8,128)}, f32[8,72,160]{2,1,0:T(8,128)}, f32[8,8,72,72]{3,2,1,0:T(8,128)S(1)},...) while((s32[]{:T(128)}, f32[10,72,160]{2,1,0:T(8,128)}, ...), condition=%wide.region_21.22_spmd, body=%wide.region_20.21_spmd.sunk | while | flops 89684256 | bytes 1932647 | solution.py:51
  776.5 55.0 %all-gather.14 = f32[64,144,16]{1,2,0:T(8,128)} all-gather(f32[1,144,16]{1,2,0:T(8,128)S(1)} %copy.134), channel_id=7, replica_groups=mesh['row'=64,'col'=4] {'row'}, dimensions={0}, use_global_device_ids=true | all-gather | bytes 599040 | tf_op jit(solution)/shard_map/all_gather | solution.py:14
  831.6 25.2 %all-gather.29.cloned.1.call-done = f32[9216,144]{1,0:T(8,128)} async-done(((f32[144,144]{1,0:T(8,128)}), f32[9216,144]{1,0:T(8,128)}) %all-gather.29.cloned.1.call-update) | async-done | bytes 5308432 | tf_op jit(solution)/shard_map/all_gather | solution.py:14
  856.8 77.0 %while.304 = (s32[]{:T(128)}, f32[144,16]{0,1:T(8,128)S(1)}, s32[]{:T(128)}, f32[64,144,144]{2,1,0:T(8,128)}, f32[64,144,16]{1,2,0:T(8,128)}, /*index=5*/s32[]{:T(128)}, s32[]{:T(128)}) while((s32[]{:T(128)}, f32[144,16]{0,1:T(8,128)S(1)}, s32[]{:T(128)}, f32[64,144,144]{2,1,0:T(8,128)}, f32[64,144,16]{1,2,0:T(8,128)}, ...), condition=%wide.region_23.24_spmd.clone, body=%wide.region_22.23_spmd.clone.sunk | while | flops 3990532 | bytes 226911 | solution.py:25
  933.9 27.9 %while.295 = (s32[]{:T(128)}, f32[10,72,16]{1,2,0:T(8,128)S(1)}, f32[8,72,72]{2,1,0:T(8,128)}, f32[8,72,16]{1,0,2:T(8,128)}, f32[8,8,72,72]{3,2,1,0:T(8,128)S(1)...) while((s32[]{:T(128)}, f32[10,72,16]{1,2,0:T(8,128)S(1)}, ...), condition=%wide.region_25.26_spmd, body=%wide.region_24.25_spmd.sunk | while | flops 8969374 | bytes 514927 | solution.py:51
  962.8 51.1 %while.296 = (s32[]{:T(128)}, f32[10,72,160]{2,1,0:T(8,128)}, s32[8,8]{1,0:T(8,128)S(1)}, f32[8,8,72,72]{2,3,1,0:T(8,128)}, f32[8,72,72]{2,1,0:T(8,128)}, /*inde...) while((s32[]{:T(128)}, f32[10,72,160]{2,1,0:T(8,128)}, ...), condition=%wide.region_28.29_spmd, body=%wide.region_26.28_spmd.sunk | while | flops 89775392 | bytes 2047909 | solution.py:70
  972.6 3.0 scatter_fusion.2
  979.2 3.0 scatter_fusion.2
  1010.9 3.0 scatter_fusion.2
  1015.8 53.5 %all-gather.15 = f32[64,144,16]{1,2,0:T(8,128)} all-gather(f32[1,144,16]{1,2,0:T(8,128)S(1)} %copy.141), channel_id=9, replica_groups=mesh['row'=64,'col'=4] {'row'}, dimensions={0}, use_global_device_ids=true | all-gather | bytes 599040 | tf_op jit(solution)/shard_map/all_gather | solution.py:14
  1069.2 28.2 %all-gather.31.cloned.1.call-done = f32[9216,144]{1,0:T(8,128)} async-done(((f32[144,144]{1,0:T(8,128)}), f32[9216,144]{1,0:T(8,128)}) %all-gather.31.cloned.1.call-update) | async-done | bytes 5308432 | tf_op jit(solution)/shard_map/all_gather | solution.py:14
  1097.5 77.4 %while.305 = (s32[]{:T(128)}, f32[144,16]{0,1:T(8,128)S(1)}, s32[]{:T(128)}, f32[64,144,144]{2,1,0:T(8,128)}, f32[64,144,16]{1,2,0:T(8,128)}, /*index=5*/s32[]{:T(128)}, s32[]{:T(128)}, s32[]{:T(128)}, s32[]{:T(128)}) while((s32[]{:T(128)}, f32[144,16]{0,1:T(8,128)S(1)}, s32[]{:T(128)}, f32[64,144,144]{2,1,0:T(8,128)}, ...), condition=%wide.region_30.31_spmd.clone, body=%wide.region_29.30_spmd.clone.sunk | while | flops 3990536 | bytes 226973 | solution.py:25
  1175.1 22.5 %while.297 = (s32[]{:T(128)}, f32[10,72,16]{1,2,0:T(8,128)S(1)}, f32[8,72,16]{1,0,2:T(8,128)S(1)}, s32[8,8]{1,0:T(8,128)S(1)}, f32[8,8,72,72]{3,2,1,0:T(8,128)S(...) while((s32[]{:T(128)}, f32[10,72,16]{1,2,0:T(8,128)S(1)}, ...), condition=%wide.region_33.34_spmd, body=%wide.region_31.33_spmd.sunk | while | flops 8977570 | bytes 520081 | solution.py:70
  1197.8 123.7 %psum.52 = f32[16]{0:T(128)S(1)} all-reduce(f32[16]{0:T(128)S(1)} %multiply_reduce_fusion.2), channel_id=1, replica_groups=mesh['row'=64,'col'=4] {'row'}, use_global_device_ids=true, to_apply=%region_35.36 | all-reduce | flops 16 | bytes 128 | tf_op jit(solution)/shard_map/psum | solution.py:141
  1322.1 9.9 all_gather.95
  1333.6 7.8 collective-permute-start.2
  1343.2 43.1 %all-reduce.21.cloned.1.call-done = f32[8,72,64]{1,0,2:T(8,128)} async-done(((f32[8,72,64]{1,0,2:T(8,128)}), f32[8,72,64]{1,0,2:T(8,128)}) %all-reduce.21.cloned.1.call-update) | async-done | bytes 147472 | tf_op jit(solution)/shard_map/psum | solution.py:133
  1387.3 5.8 collective-permute-start.3
  1400.3 21.5 reduce-scatter.5.cloned.1.call-done
  1422.9 126.8 %psum.54 = f32[16]{0:T(128)S(1)} all-reduce(f32[16]{0:T(128)S(1)} %get-tuple-element.3800), channel_id=1, replica_groups=mesh['row'=64,'col'=4] {'row'}, use_global_device_ids=true, to_apply=%region_39.40 | all-reduce | flops 16 | bytes 128 | tf_op jit(solution)/shard_map/psum | solution.py:157
  1551.4 50.2 %while.298 = (s32[]{:T(128)}, f32[10,72,160]{2,1,0:T(8,128)}, f32[8,72,72]{2,1,0:T(8,128)}, f32[8,72,160]{2,1,0:T(8,128)}, f32[8,8,72,72]{3,2,1,0:T(8,128)S(1)},...) while((s32[]{:T(128)}, f32[10,72,160]{2,1,0:T(8,128)}, ...), condition=%wide.region_41.42_spmd, body=%wide.region_40.41_spmd.sunk | while | flops 89684256 | bytes 1932647 | solution.py:51
  1604.4 55.1 %all-gather.16 = f32[64,144,16]{1,2,0:T(8,128)} all-gather(f32[1,144,16]{1,2,0:T(8,128)S(1)} %copy.155), channel_id=11, replica_groups=mesh['row'=64,'col'=4] {'row'}, dimensions={0}, use_global_device_ids=true | all-gather | bytes 599040 | tf_op jit(solution)/shard_map/all_gather | solution.py:14
  1659.5 26.2 %all-gather.33.cloned.1.call-done = f32[9216,144]{1,0:T(8,128)} async-done(((f32[144,144]{1,0:T(8,128)}), f32[9216,144]{1,0:T(8,128)}) %all-gather.33.cloned.1.call-update) | async-done | bytes 5308432 | tf_op jit(solution)/shard_map/all_gather | solution.py:14
  1685.7 77.0 %while.306 = (s32[]{:T(128)}, f32[144,16]{0,1:T(8,128)S(1)}, s32[]{:T(128)}, f32[64,144,144]{2,1,0:T(8,128)}, f32[64,144,16]{1,2,0:T(8,128)}, /*index=5*/s32[]{:T(128)}, s32[]{:T(128)}) while((s32[]{:T(128)}, f32[144,16]{0,1:T(8,128)S(1)}, s32[]{:T(128)}, f32[64,144,144]{2,1,0:T(8,128)}, f32[64,144,16]{1,2,0:T(8,128)}, ...), condition=%wide.region_43.44_spmd.clone, body=%wide.region_42.43_spmd.clone.sunk | while | flops 3990532 | bytes 226911 | solution.py:25
  1762.8 21.0 while.299
  1785.5 50.1 %while.300 = (s32[]{:T(128)}, f32[10,72,160]{2,1,0:T(8,128)}, s32[8,8]{1,0:T(8,128)S(1)}, f32[8,8,72,72]{2,3,1,0:T(8,128)}, f32[8,72,72]{2,1,0:T(8,128)}, /*inde...) while((s32[]{:T(128)}, f32[10,72,160]{2,1,0:T(8,128)}, ...), condition=%wide.region_48.49_spmd, body=%wide.region_46.48_spmd.sunk | while | flops 89775392 | bytes 2047909 | solution.py:70
  1837.4 54.6 %all-gather.17 = f32[64,144,16]{1,2,0:T(8,128)} all-gather(f32[1,144,16]{1,2,0:T(8,128)S(1)} %copy.162), channel_id=13, replica_groups=mesh['row'=64,'col'=4] {'row'}, dimensions={0}, use_global_device_ids=true | all-gather | bytes 599040 | tf_op jit(solution)/shard_map/all_gather | solution.py:14
  1892.0 27.3 %all-gather.35.cloned.1.call-done = f32[9216,144]{1,0:T(8,128)} async-done(((f32[144,144]{1,0:T(8,128)}), f32[9216,144]{1,0:T(8,128)}) %all-gather.35.cloned.1.call-update) | async-done | bytes 5308432 | tf_op jit(solution)/shard_map/all_gather | solution.py:14
  1919.3 77.4 %while.307 = (s32[]{:T(128)}, f32[144,16]{0,1:T(8,128)S(1)}, s32[]{:T(128)}, f32[64,144,144]{2,1,0:T(8,128)}, f32[64,144,16]{1,2,0:T(8,128)}, /*index=5*/s32[]{:T(128)}, s32[]{:T(128)}, s32[]{:T(128)}, s32[]{:T(128)}) while((s32[]{:T(128)}, f32[144,16]{0,1:T(8,128)S(1)}, s32[]{:T(128)}, f32[64,144,144]{2,1,0:T(8,128)}, ...), condition=%wide.region_50.51_spmd.clone, body=%wide.region_49.50_spmd.clone.sunk | while | flops 3990536 | bytes 226973 | solution.py:25
  1996.9 22.5 %while.301 = (s32[]{:T(128)}, f32[10,72,16]{1,2,0:T(8,128)S(1)}, f32[8,72,16]{1,0,2:T(8,128)S(1)}, s32[8,8]{1,0:T(8,128)S(1)}, f32[8,8,72,72]{3,2,1,0:T(8,128)S(...) while((s32[]{:T(128)}, f32[10,72,16]{1,2,0:T(8,128)S(1)}, ...), condition=%wide.region_53.54_spmd, body=%wide.region_51.53_spmd.sunk | while | flops 8977570 | bytes 520081 | solution.py:70
  2019.7 123.7 %psum.55 = f32[16]{0:T(128)S(1)} all-reduce(f32[16]{0:T(128)S(1)} %multiply_reduce_fusion), channel_id=1, replica_groups=mesh['row'=64,'col'=4] {'row'}, use_global_device_ids=true, to_apply=%region_55.56 | all-reduce | flops 16 | bytes 128 | tf_op jit(solution)/shard_map/psum | solution.py:141
  (1534 shorter events, 940.7 us)
Async XLA Ops:
  7.2 496.4 %copy-start = (f32[8,2,72,72]{3,2,1,0:T(8,128)S(1)}, f32[8,2,72,72]{3,2,1,0:T(8,128)}, u32[]{:S(2)}) copy-start(f32[8,2,72,72]{3,2,1,0:T(8,128)} %param.48) | copy-start | bytes 995332
  7.2 4.5 copy-start.17
  7.2 4.6 copy-start.27
  7.2 5.5 copy-start.1
  7.2 146.9 %all-gather.25.cloned.1.call-start = ((), (), s32[]{:S(2)}) async-start(), calls=%async_computation.6 | async-start | bytes 9584640 | tf_op jit(solution)/shard_map/all_gather | solution.py:14
  9.9 0.9 copy-start.2
  64.7 328.9 %all-gather.27.cloned.1.call-start = ((), (), s32[]{:S(2)}) async-start(), calls=%async_computation.7 | async-start | bytes 9584640 | tf_op jit(solution)/shard_map/all_gather | solution.py:14
  257.9 1.0 copy-start.19
  311.7 243.5 %all-reduce.19.cloned.1.call-start = ((), (), s32[]{:S(2)}) async-start(), calls=%async_computation.2 | async-start | bytes 524288 | tf_op jit(solution)/shard_map/psum | solution.py:133
  311.9 192.3 %copy-start.23 = (s32[8,2]{0,1:T(2,128)}, s32[8,2]{0,1:T(2,128)S(1)}, u32[]{:S(2)}) copy-start(s32[8,2]{0,1:T(2,128)S(1)} %copy.121) | copy-start | bytes 196
  312.8 191.5 %copy-start.25 = (f32[8,2]{0,1:T(2,128)}, f32[8,2]{0,1:T(2,128)S(1)}, u32[]{:S(2)}) copy-start(f32[8,2]{0,1:T(2,128)S(1)} %copy.122) | copy-start | bytes 196
  493.2 99.1 %copy-start.3 = (f32[8,72,16]{1,2,0:T(8,128)}, f32[8,72,16]{1,2,0:T(8,128)S(1)}, u32[]{:S(2)}) copy-start(f32[8,72,16]{1,2,0:T(8,128)S(1)} %get-tuple-element.3227) | copy-start | bytes 110596
  505.2 6.2 collective-permute-start
  512.0 80.3 %reduce-scatter.3.cloned.1.call-start = ((), (), s32[]{:S(2)}) async-start(), calls=%async_computation.3 | async-start | bytes 327680 | tf_op jit(solution)/shard_map/reduce_scatter | solution.py:135
  556.1 0.7 copy-start.6
  556.9 8.1 collective-permute-start.1
  565.0 5.3 copy-start.18
  567.5 2.9 copy-start.13
  570.2 286.6 %all-gather.29.cloned.1.call-start = ((), (), s32[]{:S(2)}) async-start(), calls=%async_computation.8 | async-start | bytes 9584640 | tf_op jit(solution)/shard_map/all_gather | solution.py:14
  720.2 0.5 copy-start.32
  720.7 0.5 copy-start.28
  721.3 1.0 copy-start.10
  774.4 323.1 %all-gather.31.cloned.1.call-start = ((), (), s32[]{:S(2)}) async-start(), calls=%async_computation.9 | async-start | bytes 9584640 | tf_op jit(solution)/shard_map/all_gather | solution.py:14
  961.8 1.0 copy-start.21
  1015.6 370.7 %all-reduce.21.cloned.1.call-start = ((), (), s32[]{:S(2)}) async-start(), calls=%async_computation.4 | async-start | bytes 524288 | tf_op jit(solution)/shard_map/psum | solution.py:133
  1175.0 22.5 %copy-start.11 = (f32[8,72,16]{1,0,2:T(8,128)S(1)}, f32[8,72,16]{1,0,2:T(8,128)}, u32[]{:S(2)}) copy-start(f32[8,72,16]{1,0,2:T(8,128)} %get-tuple-element.5141) | copy-start | bytes 110596
  1175.0 146.4 %copy-start.33 = (f32[16]{0:T(128)S(1)}, f32[16]{0:T(128)}, u32[]{:S(2)}) copy-start(f32[16]{0:T(128)} %copy-done.32) | copy-start | bytes 196
  1175.0 147.0 %copy-start.4 = (f32[8,72,16]{1,2,0:T(8,128)S(1)}, f32[8,72,16]{1,2,0:T(8,128)}, u32[]{:S(2)}) copy-start(f32[8,72,16]{1,2,0:T(8,128)} %copy-done.3) | copy-start | bytes 110596
  1175.1 157.6 %copy-start.24 = (s32[8,2]{0,1:T(2,128)S(1)}, s32[8,2]{0,1:T(2,128)}, u32[]{:S(2)}) copy-start(s32[8,2]{0,1:T(2,128)} %copy-done.23) | copy-start | bytes 196
  1175.1 157.6 %copy-start.26 = (f32[8,2]{0,1:T(2,128)S(1)}, f32[8,2]{0,1:T(2,128)}, u32[]{:S(2)}) copy-start(f32[8,2]{0,1:T(2,128)} %copy-done.25) | copy-start | bytes 196
  1321.4 0.6 copy-start.30
  1322.1 9.9 copy-start.7
  1333.6 8.7 collective-permute-start.2
  1342.4 0.7 copy-start.14
  1343.1 78.7 %reduce-scatter.5.cloned.1.call-start = ((), (), s32[]{:S(2)}) async-start(), calls=%async_computation.5 | async-start | bytes 327680 | tf_op jit(solution)/shard_map/reduce_scatter | solution.py:135
  1387.3 7.1 collective-permute-start.3
  1396.0 25.8 %copy-start.8 = (f32[8,72,16]{1,0,2:T(8,128)S(1)}, f32[8,72,16]{1,0,2:T(8,128)}, u32[]{:S(2)}) copy-start(f32[8,72,16]{1,0,2:T(8,128)} %copy-done.7) | copy-start | bytes 110596
  1396.0 154.3 %copy-start.12 = (f32[8,72,16]{1,0,2:T(8,128)S(1)}, f32[8,72,16]{1,0,2:T(8,128)}, u32[]{:S(2)}) copy-start(f32[8,72,16]{1,0,2:T(8,128)} %get-tuple-element.5141) | copy-start | bytes 110596
  1398.7 287.0 %all-gather.33.cloned.1.call-start = ((), (), s32[]{:S(2)}) async-start(), calls=%async_computation.10 | async-start | bytes 9584640 | tf_op jit(solution)/shard_map/all_gather | solution.py:14
  1550.4 1.0 copy-start.15
  1603.4 315.9 %all-gather.35.cloned.1.call-start = ((), (), s32[]{:S(2)}) async-start(), calls=%async_computation.11 | async-start | bytes 9584640 | tf_op jit(solution)/shard_map/all_gather | solution.py:14
  1783.8 0.7 copy-start.22
  1784.5 1.0 copy-start.20
  1996.9 22.6 %copy-start.16 = (f32[8,72,16]{1,0,2:T(8,128)S(1)}, f32[8,72,16]{1,0,2:T(8,128)}, u32[]{:S(2)}) copy-start(f32[8,72,16]{1,0,2:T(8,128)} %copy-done.15) | copy-start | bytes 110596
  1996.9 146.4 %copy-start.31 = (f32[16]{0:T(128)S(1)}, f32[16]{0:T(128)}, u32[]{:S(2)}) copy-start(f32[16]{0:T(128)} %copy-done.30) | copy-start | bytes 196
  1996.9 146.4 %copy-start.5 = (f32[8,72,16]{1,2,0:T(8,128)S(1)}, f32[8,72,16]{1,2,0:T(8,128)}, u32[]{:S(2)}) copy-start(f32[8,72,16]{1,2,0:T(8,128)} %copy-done.3) | copy-start | bytes 110596
  1996.9 146.4 %copy-start.9 = (f32[8,72,16]{1,0,2:T(8,128)S(1)}, f32[8,72,16]{1,0,2:T(8,128)}, u32[]{:S(2)}) copy-start(f32[8,72,16]{1,0,2:T(8,128)} %copy-done.7) | copy-start | bytes 110596
  1996.9 146.4 %copy-start.29 = (f32[16]{0:T(128)S(1)}, f32[16]{0:T(128)}, u32[]{:S(2)}) copy-start(f32[16]{0:T(128)} %copy-done.28) | copy-start | bytes 196
Sparse Core Ops, SparseCore 0:
  64.9 89.2 all-gather.24
  311.8 81.8 all-gather.26
  512.1 42.9 all-reduce.18
  570.3 21.9 reduce-scatter.2
  774.5 82.2 all-gather.28
  1015.8 81.6 all-gather.30
  1343.3 42.9 all-reduce.20
  1398.8 22.9 reduce-scatter.4
  1603.5 82.1 all-gather.32
  1837.5 81.8 all-gather.34
where the time goes:
time: 2170 us; the launch traced here: 2150 us
  blocking collectives  852 us (39%)
  matrix products  680 us (31%)
  waiting for transfers between devices  292 us (13%)
  local copies, waits for them, and re-layouts  170 us (8%)
  other arithmetic  98.6 us (5%)
  starting transfers between devices  24.4 us (1%)
    dot_general x384, matrix products, compose(): jnp.dot(later[0], earlier[1], precision=HIGH) + later[1]  446 us
    psum x3, blocking collectives, global_dot(): return lax.psum(jnp.sum(left * right, axis=(0, 1)), 'row')  374 us
    all_gather x6, blocking collectives, carried_in(): everything = jax.tree.map(lambda part: lax.all_gather(part, axis), x)  331 us
    all_gather x6, waiting for transfers between devices, carried_in(): everything = jax.tree.map(lambda part: lax.all_gather(part, axis), x)  160 us
    psum x1, blocking collectives, per_device(): alpha = energy / lax.psum(jnp.sum(direction * image, axis=(0, 1)), 'row')  127 us
    scatter-add x48, other arithmetic, retreat(): carried = carried.at[local_slots[row]].add(shares)  87.5 us
    psum x2, waiting for transfers between devices, system_times(): inner = lax.psum(partial_value, 'col') + every  86.1 us
    dot_general x48, matrix products, advance(): jnp.einsum('kab,kbc->ac', factor_lower[row], picked, precision=HIGH)  65.3 us
  transfers between devices with their start and end apart: 14, of which 13 were waited for; matrix products, arithmetic and copies ran while one was open for 1% of the time, Pallas kernels for 0%

commit v1 on v0

v1 whole, which is shorter than its diff:
```python
import functools

import jax
import jax.numpy as jnp
from jax import lax
from jax.experimental import pallas as pl
from jax.experimental.pallas import tpu as pltpu
from jax.sharding import PartitionSpec as P

ITERS = 2
GROUP = 8
BLK = 72
ROWS = 8
PAD = 128
WIDE = ROWS * PAD
RIM = 2 * PAD
F32 = jnp.float32
BF16 = jnp.bfloat16
MESH = pl.DeviceIdType.MESH


def split(x):
    high = x.astype(BF16)
    return high, (x - high.astype(F32)).astype(BF16)


def dot(a, b, nt):
    return lax.dot_general(
        a, b, (((1,), (1 if nt else 0,)), ((), ())), preferred_element_type=F32
    )


def stacked(v):
    high, low = split(v)
    return jnp.concatenate([high, low], axis=0)


def few(vs, high, low, nt):
    rows = vs.shape[0] // 2
    both = dot(vs, high, nt)
    return both[:rows] + both[rows:] + dot(vs[:rows], low, nt)


def many(a, b, nt=False):
    return dot(a[0], b[0], nt) + (dot(a[0], b[1], nt) + dot(a[1], b[0], nt))


def kernel(
    span, spans, cols, mask_ref, rhs_ref, sysl_ref, sysd_ref, fac_ref, dinv_ref,
    sol_ref, res_ref, dir_ref,
    dense, xh, xl, lh, ll, dh, dl, gathered, abuf, bbuf, ah, al,
    mh, ml, rh, rl, nh, nl, ph, pq, m2h, m2l, n2h, n2l, ex, nbs, nbr,
    col_send, col_recv, a_send, a_recv, b_send, b_recv, ex_send, ex_recv, nb_send, nb_recv,
):
    row, col = lax.axis_index("row"), lax.axis_index("col")
    total = span * spans
    outer, inner = row // span, row % span
    share = sysl_ref.shape[1]
    columns = rhs_ref.shape[0]

    def inner_peer(t):
        return (outer * span + (inner + t) % span, col)

    def outer_peer(t):
        return (((outer + t) % spans) * span + inner, col)

    up, down = ((row + 1) % total, col), ((row + total - 1) % total, col)

    barrier = pltpu.get_barrier_semaphore()
    greeted = (
        [inner_peer(t) for t in range(1, span)]
        + [outer_peer(t) for t in range(1, spans)]
        + [(row, (col + t) % cols) for t in range(1, cols)]
        + [up, down]
    )
    for peer in greeted:
        pl.semaphore_signal(barrier, inc=1, device_id=peer, device_id_type=MESH)
    pl.semaphore_wait(barrier, len(greeted))

    sends = []

    def spread(buf, slot, peers, count, send_sem, recv_sem):
        for peer in peers:
            pltpu.make_async_remote_copy(
                src_ref=buf.at[slot], dst_ref=buf.at[slot], send_sem=send_sem,
                recv_sem=recv_sem, device_id=peer, device_id_type=MESH,
            ).start()
        every = pltpu.make_async_remote_copy(
            src_ref=buf.at[pl.ds(0, count)], dst_ref=buf.at[pl.ds(0, count)],
            send_sem=send_sem, recv_sem=recv_sem, device_id=up, device_id_type=MESH,
        )
        sends.append(every)
        return every

    for t in range(1, cols):
        pltpu.make_async_remote_copy(
            src_ref=sysl_ref, dst_ref=gathered.at[col], send_sem=col_send, recv_sem=col_recv,
            device_id=(row, (col + t) % cols), device_id_type=MESH,
        ).start()
    col_every = pltpu.make_async_remote_copy(
        src_ref=gathered.at[pl.ds(0, cols - 1)], dst_ref=gathered.at[pl.ds(0, cols - 1)],
        send_sem=col_send, recv_sem=col_recv, device_id=up, device_id_type=MESH,
    )
    sends.append(col_every)
    gathered[col] = sysl_ref[...]

    def place(block_of):
        def one(i, carry):
            blocks = [block_of(i, k) for k in range(8)]
            at = pl.multiple_of(i * PAD, PAD)
            for s in range(ROWS + 2):
                value = mask_ref[(i * 8) * (ROWS + 2) + s] * blocks[0]
                for k in range(1, 8):
                    value += mask_ref[(i * 8 + k) * (ROWS + 2) + s] * blocks[k]
                dense[pl.ds(at, BLK), s * PAD : s * PAD + BLK] = value
            return carry

        lax.fori_loop(0, ROWS, one, 0)

    def padded(block):
        wide = jnp.concatenate([block, jnp.zeros((BLK, PAD - BLK), F32)], axis=1)
        return jnp.concatenate([wide, jnp.zeros((PAD - BLK, PAD), F32)], axis=0)

    dense[...] = jnp.zeros_like(dense)
    place(lambda i, k: fac_ref[i, k])

    for i in range(ROWS):
        inverse = padded(dinv_ref[i])
        width = RIM + i * PAD
        given = dense[i * PAD : (i + 1) * PAD, :width]
        scaled = many(split(inverse), split(given))
        edge = scaled[:, :RIM]
        if i > 0:
            step = many(
                split(scaled[:, RIM:]), (xh[: i * PAD, :width], xl[: i * PAD, :width])
            )
            edge = edge - step[:, :RIM]
            body = [edge, -step[:, RIM:], inverse]
        else:
            body = [edge, inverse]
        if i < ROWS - 1:
            body.append(jnp.zeros((PAD, WIDE - (i + 1) * PAD), F32))
        high, low = split(jnp.concatenate(body, axis=1))
        xh[i * PAD : (i + 1) * PAD, :] = high
        xl[i * PAD : (i + 1) * PAD, :] = low
        if i >= ROWS - 2:
            at = (i - ROWS + 2) * BLK
            abuf[inner, at : at + BLK, :] = -edge[:BLK, :]

    a_every = spread(
        abuf, inner, [inner_peer(t) for t in range(1, span)], span - 1, a_send, a_recv
    )

    col_every.wait_recv()
    place(lambda i, k: gathered[k // share, i, k % share])
    for i in range(ROWS):
        high, low = split(dense[i * PAD : (i + 1) * PAD, :])
        lh[i * PAD : (i + 1) * PAD, :] = high
        ll[i * PAD : (i + 1) * PAD, :] = low
        high, low = split(padded(sysd_ref[i]))
        dh[i] = high
        dl[i] = low

    def spread_rows(value):
        gap = jnp.zeros((PAD - BLK, RIM), F32)
        return jnp.concatenate([value[:BLK], gap, value[BLK:], gap], axis=0)

    r_iota = lax.broadcasted_iota(jnp.int32, (RIM, RIM), 0)
    c_iota = lax.broadcasted_iota(jnp.int32, (RIM, RIM), 1)
    eye = jnp.where((r_iota == c_iota) & (c_iota % PAD < BLK), 1.0, 0.0).astype(F32)

    def put(refs, s, value):
        high, low = split(value)
        refs[0][s] = high
        refs[1][s] = low

    def get(refs, s):
        return refs[0][s], refs[1][s]

    a_refs, m_refs, r_refs, n_refs, p_refs = (ah, al), (mh, ml), (rh, rl), (nh, nl), (ph, pq)
    m2_refs, n2_refs = (m2h, m2l), (n2h, n2l)

    def flag(condition):
        return jnp.where(condition, 1.0, 0.0).astype(F32)

    a_every.wait_recv()
    for s in range(span):
        put(a_refs, s, spread_rows(abuf[s]))
    put(m_refs, span - 1, jnp.zeros((RIM, RIM), F32))
    put(r_refs, span - 1, eye)
    put(n_refs, 0, jnp.zeros((RIM, RIM), F32))
    put(p_refs, 0, eye)

    def chain(t, carry):
        s = span - 1 - t
        right = get(a_refs, s)
        put(m_refs, s - 1, many(get(m_refs, s), right) + flag(s == inner) * eye)
        put(r_refs, s - 1, many(get(r_refs, s), right))
        left = get(a_refs, t)
        put(n_refs, t + 1, many(left, get(n_refs, t)) + flag(t == inner) * eye)
        put(p_refs, t + 1, many(left, get(p_refs, t)))
        return carry

    lax.fori_loop(0, span - 1, chain, 0)
    across = many(get(a_refs, span - 1), get(p_refs, span - 1))
    bbuf[outer, :BLK, :] = across[:BLK]
    bbuf[outer, BLK:, :] = across[PAD : PAD + BLK]
    b_every = spread(
        bbuf, outer, [outer_peer(t) for t in range(1, spans)], spans - 1, b_send, b_recv
    )

    lane = lax.broadcasted_iota(jnp.int32, (columns, RIM), 1)

    def with_sum(value, sums):
        return jnp.where(lane == BLK, sums, jnp.where(lane % PAD < BLK, value, 0.0))

    def lane_sum(value):
        return jnp.sum(value, axis=1, keepdims=True)

    def exchange(phase, value, level):
        buf = ex.at[phase]
        if level == 0:
            buf[inner] = value
            peers, slot, count = [inner_peer(t) for t in range(1, span)], inner, span - 1
        else:
            buf[outer] = value
            peers, slot, count = [outer_peer(t) for t in range(1, spans)], outer, spans - 1
        return spread(buf, slot, peers, count, ex_send.at[phase], ex_recv.at[phase])

    def collect(phase, count, refs, nt):
        value = jnp.zeros((columns, RIM), F32)
        for s in range(count):
            value += few(stacked(ex[phase, s]), *get(refs, s), nt)
        return value

    def sums_of(phase, count):
        value = ex[phase, 0]
        for s in range(1, count):
            value += ex[phase, s]
        return lane_sum(jnp.where(lane == BLK, value, 0.0))

    tail = WIDE - RIM

    def forward_first(phase, source, sums):
        vs = stacked(source)
        rim = few(vs, xh[tail:, RIM:], xl[tail:, RIM:], True)
        wait = exchange(phase, with_sum(rim, sums), 0)
        parts = []
        for i in range(3):
            a, b = i * RIM, (i + 1) * RIM
            parts.append(few(vs[:, :b], xh[a:b, RIM : RIM + b], xl[a:b, RIM : RIM + b], True))
        local = jnp.concatenate(parts + [rim], axis=1)
        wait.wait_recv()
        value = collect(phase, span, r_refs, True)
        wait = exchange(phase + 1, with_sum(value, sums_of(phase, span)), 1)
        near = collect(phase, span, m_refs, True)
        return local, near, wait

    def forward_last(phase, local, near, wait):
        wait.wait_recv()
        entering = near + collect(phase + 1, spans, m2_refs, True)
        moved = few(stacked(entering), xh[:, :RIM], xl[:, :RIM], True)
        return local - moved, sums_of(phase + 1, spans)

    def backward(phase, source):
        vs = stacked(source)
        rim = few(vs, xh[:, :RIM], xl[:, :RIM], False)
        wait = exchange(phase, with_sum(rim, lane_sum(source * source)), 0)
        parts = []
        for i in range(4):
            a, b = i * RIM, (i + 1) * RIM
            parts.append(
                few(vs[:, a:], xh[a:, RIM + a : RIM + b], xl[a:, RIM + a : RIM + b], False)
            )
        local = jnp.concatenate(parts, axis=1)
        wait.wait_recv()
        value = collect(phase, span, p_refs, False)
        wait = exchange(phase + 1, with_sum(value, sums_of(phase, span)), 1)
        near = collect(phase, span, n_refs, False)
        wait.wait_recv()
        entering = near + collect(phase + 1, spans, n2_refs, False)
        moved = few(stacked(entering), xh[tail:, RIM:], xl[tail:, RIM:], False)
        return local - moved, sums_of(phase + 1, spans)

    def system_times(step, vector):
        vs = stacked(vector)
        falling = few(vs, lh[:, :RIM], ll[:, :RIM], False)
        last = vector[:, tail:] + few(
            vs[:, tail:], lh[tail:, RIM + tail :], ll[tail:, RIM + tail :], False
        )
        nbs[step, 0] = falling
        nbs[step, 1] = last
        copies = []
        for way, peer in ((0, down), (1, up)):
            copy = pltpu.make_async_remote_copy(
                src_ref=nbs.at[step, way], dst_ref=nbr.at[step, way],
                send_sem=nb_send.at[step, way], recv_sem=nb_recv.at[step, way],
                device_id=peer, device_id_type=MESH,
            )
            copy.start()
            copies.append(copy)
            sends.append(copy)
        parts = []
        for i in range(3):
            a, b = i * RIM, (i + 1) * RIM
            parts.append(
                vector[:, a:b]
                + few(vs[:, a:], lh[a:, RIM + a : RIM + b], ll[a:, RIM + a : RIM + b], False)
            )
        upper = jnp.concatenate(parts + [last], axis=1)
        us = stacked(upper)
        parts = []
        for i in range(4):
            a, b = i * RIM, (i + 1) * RIM
            parts.append(few(us[:, :b], lh[a:b, RIM : RIM + b], ll[a:b, RIM : RIM + b], True))
        diagonal = [
            few(vs[:, i * PAD : (i + 1) * PAD], dh[i], dl[i], False) for i in range(ROWS)
        ]
        image = upper + jnp.concatenate(parts, axis=1) + jnp.concatenate(diagonal, axis=1)
        copies[0].wait_recv()
        coming = nbr[step, 0] * flag(row < total - 1)
        corner = coming + few(
            stacked(coming), lh[tail:, RIM + tail :], ll[tail:, RIM + tail :], True
        )
        copies[1].wait_recv()
        before = (nbr[step, 1] + falling) * flag(row > 0)
        image = image + few(stacked(before), lh[:, :RIM], ll[:, :RIM], True)
        return jnp.concatenate([image[:, :tail], image[:, tail:] + corner], axis=1)

    residual = rhs_ref[...]
    state = forward_first(0, residual, jnp.zeros((columns, 1), F32))

    b_every.wait_recv()
    for s in range(spans):
        put(a_refs, s, spread_rows(bbuf[s]))
    mine_p = ph[inner].astype(F32) + pq[inner].astype(F32)
    mine_r = rh[inner].astype(F32) + rl[inner].astype(F32)
    put(m2_refs, spans - 1, jnp.zeros((RIM, RIM), F32))
    put(n2_refs, 0, jnp.zeros((RIM, RIM), F32))

    def outer_chain(t, carry):
        s = spans - 1 - t
        put(m2_refs, s - 1, many(get(m2_refs, s), get(a_refs, s)) + flag(s == outer) * mine_p)
        put(n2_refs, t + 1, many(get(a_refs, t), get(n2_refs, t)) + flag(t == outer) * mine_r)
        return carry

    lax.fori_loop(0, spans - 1, outer_chain, 0)

    solved, _ = forward_last(0, *state)
    direction, energy = backward(2, solved)
    answer = jnp.zeros_like(residual)
    for step in range(ITERS):
        phase = 4 * (step + 1)
        image = system_times(step, direction)
        state = forward_first(phase, image, lane_sum(direction * image))
        change, curvature = forward_last(phase, *state)
        alpha = energy / curvature
        answer = answer + alpha * direction
        residual = residual - alpha * image
        solved = solved - alpha * change
        precond, energy_next = backward(phase + 2, solved)
        direction = precond + (energy_next / energy) * direction
        energy = energy_next

    sol_ref[...] = answer
    res_ref[...] = residual
    dir_ref[...] = direction
    for copy in sends:
        copy.wait_send()


def per_device(
    spans, cols, rhs, system_lower, system_diag, factor_lower, diag_inverse, neighbours, counts
):
    rows, width, columns = rhs.shape
    places = neighbours - lax.axis_index("row") * rows + 2
    live = jnp.arange(8, dtype=jnp.int32)[None, :] < counts[:, None]
    mask = (places[:, :, None] == jnp.arange(rows + 2, dtype=jnp.int32)) & live[:, :, None]
    mask = mask.astype(F32).reshape(-1)
    turned = jnp.pad(jnp.transpose(rhs, (2, 0, 1)), ((0, 0), (0, 0), (0, PAD - width)))
    turned = turned.reshape(columns, WIDE)
    vmem = pl.BlockSpec(memory_space=pltpu.VMEM)
    phases = 4 * (ITERS + 1)
    half = lambda: pltpu.VMEM((GROUP, RIM, RIM), BF16)
    most = max(GROUP, spans)
    tall = lambda: pltpu.VMEM((most, RIM, RIM), BF16)
    dma = pltpu.SemaphoreType.DMA
    outs = pl.pallas_call(
        functools.partial(kernel, GROUP, spans, cols),
        out_shape=[jax.ShapeDtypeStruct((columns, WIDE), F32)] * 3,
        in_specs=[pl.BlockSpec(memory_space=pltpu.SMEM)] + [vmem] * 5,
        out_specs=[vmem] * 3,
        scratch_shapes=[
            pltpu.VMEM((WIDE, RIM + WIDE), F32),
            pltpu.VMEM((WIDE, RIM + WIDE), BF16),
            pltpu.VMEM((WIDE, RIM + WIDE), BF16),
            pltpu.VMEM((WIDE, RIM + WIDE), BF16),
            pltpu.VMEM((WIDE, RIM + WIDE), BF16),
            pltpu.VMEM((ROWS, PAD, PAD), BF16),
            pltpu.VMEM((ROWS, PAD, PAD), BF16),
            pltpu.VMEM((cols,) + system_lower.shape, F32),
            pltpu.VMEM((GROUP, 2 * BLK, RIM), F32),
            pltpu.VMEM((spans, 2 * BLK, RIM), F32),
            tall(), tall(),
            half(), half(), half(), half(), half(), half(), half(), half(),
            tall(), tall(), tall(), tall(),
            pltpu.VMEM((phases, most, columns, RIM), F32),
            pltpu.VMEM((ITERS, 2, columns, RIM), F32),
            pltpu.VMEM((ITERS, 2, columns, RIM), F32),
            dma, dma, dma, dma, dma, dma,
            dma((phases,)), dma((phases,)), dma((ITERS, 2)), dma((ITERS, 2)),
        ],
        compiler_params=pltpu.CompilerParams(
            collective_id=0, has_side_effects=True, vmem_limit_bytes=60 * 1024 * 1024
        ),
    )(mask, turned, system_lower, system_diag, factor_lower, diag_inverse)

    def back(value):
        return jnp.transpose(value.reshape(columns, rows, PAD)[:, :, :width], (1, 2, 0))

    return tuple(back(value) for value in outs)


def solution(mesh):
    in_specs = (
        P("row", None, "col"),
        P("row", "col", None, None),
        P("row", None, None),
        P("row", None, None, None),
        P("row", None, None),
        P("row", None),
        P("row"),
    )
    out_specs = (P("row", None, "col"), P("row", None, "col"), P("row", None, "col"))
    return jax.shard_map(
        functools.partial(per_device, mesh.shape["row"] // GROUP, mesh.shape["col"]),
        mesh=mesh, in_specs=in_specs, out_specs=out_specs, check_vma=False,
    )
```

time: 2170 us -> 160 us (0.07)
  blocking collectives: 852 us -> 0 us
  matrix products: 680 us -> 0 us
  waiting for transfers between devices: 292 us -> 0 us
  local copies, waits for them, and re-layouts: 170 us -> 6.13 us
  Pallas kernels: 0 us -> 151 us
  other arithmetic: 98.6 us -> 1.5 us
  starting transfers between devices: 24.4 us -> 0 us
    dot_general x584 -> x0, matrix products: 680 us -> none  [the longest x384 446 us: compose(): jnp.dot(later[0], earlier[1], precision=HIGH) + later[1]]
    psum x4 -> x0, blocking collectives: 501 us -> none  [the longest x3 374 us: global_dot(): return lax.psum(jnp.sum(left * right, axis=(0, 1)), 'row')]
    all_gather x8 -> x0, blocking collectives: 351 us -> none  [the longest x6 331 us: carried_in(): everything = jax.tree.map(lambda part: lax.all_gather(part, axis), x)]
    all_gather x6 -> x0, waiting for transfers between devices: 160 us -> none  [carried_in(): everything = jax.tree.map(lambda part: lax.all_gather(part, axis), x)]
    pallas_call x0 -> x1, Pallas kernels: none -> 151 us  [per_device(): pl.pallas_call(functools.partial(kernel, GROUP, spans, cols), out_shape=[...]
    scatter-add x50 -> x0, other arithmetic: 88.3 us -> none  [the longest x48 87.5 us: retreat(): carried = carried.at[local_slots[row]].add(shares)]
    psum x2 -> x0, waiting for transfers between devices: 86.1 us -> none  [system_times(): inner = lax.psum(partial_value, 'col') + every]
    mul x96 -> x0, local copies, waits for them, and re-layouts: 66.4 us -> none  [the longest x48 33.3 us: retreat(): jnp.einsum('kab,ac->kbc', factor_lower[row], value, precision=HIGH)]
  transfers between devices with their start and end apart: 14 -> 0, of which waited for: 13 -> 0; matrix products, arithmetic and copies ran while one was open for 1% -> 0% of each run, Pallas kernels for 0% -> 0%
where the time goes in v1:
time: 160 us; the launch traced here: 159 us
  Pallas kernels  151 us (94%)
  local copies, waits for them, and re-layouts  6.13 us (4%)
    pallas_call x1, Pallas kernels, per_device(): pl.pallas_call(functools.partial(kernel, GROUP, spans, cols), out_shape=[...  151 us
    unnamed x6, local copies, waits for them, and re-layouts  4.71 us

profile of v1, /device:TPU:1, one launch (start us, length us, event | category | flops | bytes accessed | tf_op | source)
XLA Modules:
  0.0 159.4 jit_solution(2628390222824547235)
XLA Ops:
  0.6 0.7 iota_compare_fusion.1
  1.4 0.7 subtract_add_fusion
  2.1 0.1 fusion.1
  2.1 0.7 reshape.52.mask_ref
  2.9 0.9 copy.17
  3.8 0.6 copy.26
  4.4 151.1 %shard_map.94 = (f32[16,1024]{1,0:T(8,128)}, f32[16,1024]{1,0:T(8,128)}, f32[16,1024]{1,0:T(8,128)}) custom-call(f32[640]{0:T(1024)} %reshape.52.mask_ref, f32[16,1024]{1,0:T(8,128)} %bitcast.21, f32[8,2,72,72]{3,2,1,0:T(8,128)} %sysl_ref.1, f32[8,72,72]{2,1,0:T(8,128)} %sysd_ref.1, f32[8,8,72,72]{3,2,1,0:T(8,128)} %fac_ref.1, f32[8,72,72]{2,1,0:T(8,128)} %dinv_ref.1), custom_call_target="tpu_custom_call" | custom-call | tf_op jit(solution)/shard_map/pallas_call | solution.py:388
  155.6 0.9 copy.19
  156.4 0.6 copy.27
  157.1 0.9 copy.20
  157.9 0.9 copy.21
  158.8 0.7 copy_bitcast_fusion.1
  (1 shorter events, 0.0 us)

commit v2 on v1

v2 whole, which is shorter than its diff:
```python
import functools

import jax
import jax.numpy as jnp
from jax import lax
from jax.experimental import pallas as pl
from jax.experimental.pallas import tpu as pltpu
from jax.sharding import PartitionSpec as P

ITERS = 2
GROUP = 8
BLK = 72
ROWS = 8
PAD = 128
WIDE = ROWS * PAD
RIM = 2 * PAD
PACKED = BLK + 16
F32 = jnp.float32
BF16 = jnp.bfloat16
MESH = pl.DeviceIdType.MESH


def split(x):
    high = x.astype(BF16)
    return high, (x - high.astype(F32)).astype(BF16)


def dot(a, b, nt):
    return lax.dot_general(
        a, b, (((1,), (1 if nt else 0,)), ((), ())), preferred_element_type=F32
    )


def stacked(v):
    high, low = split(v)
    return jnp.concatenate([high, low], axis=0)


def few(vs, high, low, nt):
    rows = vs.shape[0] // 2
    both = dot(vs, high, nt)
    return both[:rows] + both[rows:] + dot(vs[:rows], low, nt)


def many(a, b, nt=False):
    return dot(a[0], b[0], nt) + (dot(a[0], b[1], nt) + dot(a[1], b[0], nt))


def nearest(count):
    return sorted(range(1, count), key=lambda t: min(t, count - t))


def pack(half):
    lane = lax.broadcasted_iota(jnp.int32, (BLK, PAD), 1)
    turned = pltpu.roll(half[:, PAD:], BLK, 1)
    top = jnp.where(lane < BLK, half[:, :PAD], turned)
    rest = jnp.where(lane < 16, turned, 0.0)
    first = rest[:8]
    for g in range(1, 8):
        first += pltpu.roll(rest[8 * g : 8 * g + 8], 16 * g, 1)
    return jnp.concatenate([top, first, rest[64:]], axis=0)


def unpack(packed):
    lane = lax.broadcasted_iota(jnp.int32, (BLK, PAD), 1)
    top, first, last = packed[:BLK], packed[BLK : BLK + 8], packed[BLK + 8 :]
    edge = PAD - BLK
    rest = [pltpu.roll(first, (edge - 16 * g) % PAD, 1) for g in range(8)]
    rest = jnp.concatenate(rest + [pltpu.roll(last, edge, 1)], axis=0)
    right = jnp.where(lane < edge, pltpu.roll(top, edge, 1), jnp.where(lane < BLK, rest, 0.0))
    left = jnp.where(lane < BLK, top, 0.0)
    value = jnp.concatenate([left, right], axis=1)
    return jnp.concatenate([value, jnp.zeros((PAD - BLK, RIM), F32)], axis=0)


def kernel(
    span, spans, cols, neighbours_ref, counts_ref, rhs_ref, sysl_ref, sysd_ref, fac_ref, dinv_ref,
    sol_ref, res_ref, dir_ref,
    dense, xh, xl, lh, ll, dh, dl, gathered, abuf, bbuf, ah, al,
    mh, ml, rh, rl, nh, nl, ph, pq, m2h, m2l, n2h, n2l, ex, nbs, nbr,
    col_send, col_recv, a_send, a_recv, b_send, b_recv, ex_send, ex_recv, nb_send, nb_recv,
):
    row, col = lax.axis_index("row"), lax.axis_index("col")
    total = span * spans
    outer, inner = row // span, row % span
    share = sysl_ref.shape[1]
    columns = rhs_ref.shape[1]
    chips = span // 2
    chip, core = inner // 2, inner % 2

    def at_inner(x, c):
        return ((chip + x + chips) % chips) * 2 + (core + c + 2) % 2

    def at_outer(t):
        return (outer + t + spans) % spans

    def inner_peer(x, c):
        return (outer * span + at_inner(x, c), col)

    def outer_peer(t):
        return (at_outer(t) * span + inner, col)

    inner_steps = [(x, c) for x in [0] + nearest(chips) for c in range(2)][1:]
    outer_steps = nearest(spans)
    up, down = ((row + 1) % total, col), ((row + total - 1) % total, col)
    sibling = inner_peer(0, 1)

    barrier = pltpu.get_barrier_semaphore()
    greeted = (
        [inner_peer(*t) for t in inner_steps]
        + [outer_peer(t) for t in outer_steps]
        + [(row, (col + t) % cols) for t in range(1, cols)]
        + [up, down]
    )
    for peer in greeted:
        pl.semaphore_signal(barrier, inc=1, device_id=peer, device_id_type=MESH)

    sends = []

    def remote(source, target, send_sem, recv_sem, peer):
        return pltpu.make_async_remote_copy(
            src_ref=source, dst_ref=target, send_sem=send_sem, recv_sem=recv_sem,
            device_id=peer, device_id_type=MESH,
        )

    def place(block_of):
        def one(i, carry):
            blocks = [block_of(i, k) for k in range(8)]
            at = pl.multiple_of(i * PAD, PAD)
            places = [
                jnp.where(k < counts_ref[i], neighbours_ref[i, k] - row * ROWS + 2, -1)
                for k in range(8)
            ]
            for s in range(ROWS + 2):
                value = jnp.where(places[0] == s, 1.0, 0.0) * blocks[0]
                for k in range(1, 8):
                    value += jnp.where(places[k] == s, 1.0, 0.0) * blocks[k]
                dense[pl.ds(at, BLK), s * PAD : s * PAD + BLK] = value
            return carry

        lax.fori_loop(0, ROWS, one, 0)

    def padded(block):
        wide = jnp.concatenate([block, jnp.zeros((BLK, PAD - BLK), F32)], axis=1)
        return jnp.concatenate([wide, jnp.zeros((PAD - BLK, PAD), F32)], axis=0)

    dense[...] = jnp.zeros_like(dense)
    place(lambda i, k: fac_ref[i, k])

    for i in range(ROWS):
        inverse = padded(dinv_ref[i])
        width = RIM + i * PAD
        given = dense[i * PAD : (i + 1) * PAD, :width]
        scaled = many(split(inverse), split(given))
        edge = scaled[:, :RIM]
        if i > 0:
            step = many(
                split(scaled[:, RIM:]), (xh[: i * PAD, :width], xl[: i * PAD, :width])
            )
            edge = edge - step[:, :RIM]
            body = [edge, -step[:, RIM:], inverse]
        else:
            body = [edge, inverse]
        if i < ROWS - 1:
            body.append(jnp.zeros((PAD, WIDE - (i + 1) * PAD), F32))
        high, low = split(jnp.concatenate(body, axis=1))
        xh[i * PAD : (i + 1) * PAD, :] = high
        xl[i * PAD : (i + 1) * PAD, :] = low
        if i >= ROWS - 2:
            abuf[inner, i - ROWS + 2] = pack(-edge[:BLK, :])

    pl.semaphore_wait(barrier, len(greeted))

    def hand(buf, slot, n, send, recv, peer):
        copy = remote(buf.at[slot], buf.at[slot], send.at[n], recv.at[n], peer)
        copy.start()
        sends.append(copy)

    def awaited(buf, slot, n, send, recv):
        remote(buf.at[slot], buf.at[slot], send.at[n], recv.at[n], sibling).wait_recv()

    for x in reversed(nearest(chips)):
        hand(abuf, inner, x, a_send, a_recv, inner_peer(x, 0))
    hand(abuf, inner, 0, a_send, a_recv, sibling)

    lane = lax.broadcasted_iota(jnp.int32, (columns, RIM), 1)

    def with_sum(value, sums):
        return jnp.where(lane == BLK, sums, jnp.where(lane % PAD < BLK, value, 0.0))

    def lane_sum(value):
        return jnp.sum(value, axis=1, keepdims=True)

    def get(refs, s):
        return refs[0][s], refs[1][s]

    def exchange(phase, value, level):
        buf = ex.at[phase]
        mine, steps, peer_of, count = (
            (inner, inner_steps, lambda t: inner_peer(*t), span)
            if level == 0
            else (outer, outer_steps, outer_peer, spans)
        )
        buf[mine] = value
        coming = []
        for n, t in reversed(list(enumerate(steps))):
            sems = ex_send.at[phase], ex_recv.at[phase, n]
            remote(buf.at[mine], buf.at[mine], *sems, peer_of(t)).start()
            origin = at_inner(-t[0], -t[1]) if level == 0 else at_outer(-t)
            coming.append((origin, remote(buf.at[origin], buf.at[origin], *sems, sibling)))
        every = buf.at[pl.ds(0, count - 1)]
        sends.append(remote(every, every, ex_send.at[phase], ex_recv.at[phase, 0], sibling))
        return phase, mine, value, coming[::-1]

    def collect(exchanged, refs, nt):
        phase, mine, value, coming = exchanged
        result = few(stacked(value), *get(refs, mine), nt)
        for origin, copy in coming:
            copy.wait_recv()
            arrived = ex[phase, origin]
            value = value + arrived
            result += few(stacked(arrived), *get(refs, origin), nt)
        return result, lane_sum(jnp.where(lane == BLK, value, 0.0))

    def again(exchanged, refs, nt):
        phase, mine, value, coming = exchanged
        result = few(stacked(value), *get(refs, mine), nt)
        for origin, _ in coming:
            result += few(stacked(ex[phase, origin]), *get(refs, origin), nt)
        return result

    tail = WIDE - RIM

    def forward_local(phase, source, sums):
        vs = stacked(source)
        rim = few(vs, xh[tail:, RIM:], xl[tail:, RIM:], True)
        near = exchange(phase, with_sum(rim, sums), 0)
        parts = []
        for i in range(3):
            a, b = i * RIM, (i + 1) * RIM
            parts.append(few(vs[:, :b], xh[a:b, RIM : RIM + b], xl[a:b, RIM : RIM + b], True))
        return near, jnp.concatenate(parts + [rim], axis=1)

    def across_spans(phase, near, first, second, nt):
        value, sums = collect(near, first, nt)
        far = exchange(phase, with_sum(value, sums), 1)
        return far, again(near, second, nt)

    def forward_last(far, local, entering):
        value, sums = collect(far, m2_refs, True)
        moved = few(stacked(entering + value), xh[:, :RIM], xl[:, :RIM], True)
        return local - moved, sums

    def backward(phase, source, beside=None):
        vs = stacked(source)
        rim = few(vs, xh[:, :RIM], xl[:, :RIM], False)
        near = exchange(phase, with_sum(rim, lane_sum(source * source)), 0)
        parts = []
        for i in range(4):
            a, b = i * RIM, (i + 1) * RIM
            parts.append(
                few(vs[:, a:], xh[a:, RIM + a : RIM + b], xl[a:, RIM + a : RIM + b], False)
            )
        local = jnp.concatenate(parts, axis=1)
        far, entering = across_spans(phase + 1, near, p_refs, n_refs, False)
        if beside is not None:
            beside()
        value, sums = collect(far, n2_refs, False)
        moved = few(stacked(entering + value), xh[tail:, RIM:], xl[tail:, RIM:], False)
        return local - moved, sums

    def system_times(step, vector):
        vs = stacked(vector)
        falling = few(vs, lh[:, :RIM], ll[:, :RIM], False)
        last = vector[:, tail:] + few(
            vs[:, tail:], lh[tail:, RIM + tail :], ll[tail:, RIM + tail :], False
        )
        nbs[step, 0] = falling
        nbs[step, 1] = last
        copies = []
        for way, peer in ((0, down), (1, up)):
            copy = remote(
                nbs.at[step, way], nbr.at[step, way],
                nb_send.at[step, way], nb_recv.at[step, way], peer,
            )
            copy.start()
            copies.append(copy)
            sends.append(copy)
        parts = []
        for i in range(3):
            a, b = i * RIM, (i + 1) * RIM
            parts.append(
                vector[:, a:b]
                + few(vs[:, a:], lh[a:, RIM + a : RIM + b], ll[a:, RIM + a : RIM + b], False)
            )
        upper = jnp.concatenate(parts + [last], axis=1)
        us = stacked(upper)
        parts = []
        for i in range(4):
            a, b = i * RIM, (i + 1) * RIM
            parts.append(few(us[:, :b], lh[a:b, RIM : RIM + b], ll[a:b, RIM : RIM + b], True))
        diagonal = [
            few(vs[:, i * PAD : (i + 1) * PAD], dh[i], dl[i], False) for i in range(ROWS)
        ]
        image = upper + jnp.concatenate(parts, axis=1) + jnp.concatenate(diagonal, axis=1)
        copies[0].wait_recv()
        coming = nbr[step, 0] * flag(row < total - 1)
        corner = coming + few(
            stacked(coming), lh[tail:, RIM + tail :], ll[tail:, RIM + tail :], True
        )
        copies[1].wait_recv()
        before = (nbr[step, 1] + falling) * flag(row > 0)
        image = image + few(stacked(before), lh[:, :RIM], ll[:, :RIM], True)
        return jnp.concatenate([image[:, :tail], image[:, tail:] + corner], axis=1)

    gap = jnp.zeros((columns, PAD - BLK), F32)
    residual = jnp.concatenate(
        [part for i in range(ROWS) for part in (rhs_ref[i], gap)], axis=1
    )
    near, local = forward_local(0, residual, jnp.zeros((columns, 1), F32))

    for t in range(1, cols):
        remote(
            sysl_ref, gathered.at[col], col_send, col_recv, (row, (col + t) % cols)
        ).start()
    others = gathered.at[pl.ds(0, cols - 1)]
    col_every = remote(others, others, col_send, col_recv, up)
    sends.append(col_every)
    gathered[col] = sysl_ref[...]

    def place_system():
        col_every.wait_recv()
        place(lambda i, k: gathered[k // share, i, k % share])
        for i in range(ROWS):
            high, low = split(dense[i * PAD : (i + 1) * PAD, :])
            lh[i * PAD : (i + 1) * PAD, :] = high
            ll[i * PAD : (i + 1) * PAD, :] = low
            high, low = split(padded(sysd_ref[i]))
            dh[i] = high
            dl[i] = low

    r_iota = lax.broadcasted_iota(jnp.int32, (RIM, RIM), 0)
    c_iota = lax.broadcasted_iota(jnp.int32, (RIM, RIM), 1)
    eye = jnp.where((r_iota == c_iota) & (c_iota % PAD < BLK), 1.0, 0.0).astype(F32)

    def put(refs, s, value):
        high, low = split(value)
        refs[0][s] = high
        refs[1][s] = low

    a_refs, m_refs, r_refs, n_refs, p_refs = (ah, al), (mh, ml), (rh, rl), (nh, nl), (ph, pq)
    m2_refs, n2_refs = (m2h, m2l), (n2h, n2l)

    def flag(condition):
        return jnp.where(condition, 1.0, 0.0).astype(F32)

    def unpack_all(buf, s, carry):
        put(a_refs, s, jnp.concatenate([unpack(buf[s, 0]), unpack(buf[s, 1])], axis=0))
        return carry

    for x in nearest(chips):
        origin = at_inner(-x, 0)
        awaited(abuf, origin, x, a_send, a_recv)
        hand(abuf, origin, chips + x, a_send, a_recv, sibling)
    awaited(abuf, at_inner(0, 1), 0, a_send, a_recv)
    for x in nearest(chips):
        awaited(abuf, at_inner(-x, 1), chips + x, a_send, a_recv)
    lax.fori_loop(0, span, functools.partial(unpack_all, abuf), 0)
    put(m_refs, span - 1, jnp.zeros((RIM, RIM), F32))
    put(r_refs, span - 1, eye)
    put(n_refs, 0, jnp.zeros((RIM, RIM), F32))
    put(p_refs, 0, eye)

    def chain(t, carry):
        s = span - 1 - t
        right = get(a_refs, s)
        put(m_refs, s - 1, many(get(m_refs, s), right) + flag(s == inner) * eye)
        put(r_refs, s - 1, many(get(r_refs, s), right))
        left = get(a_refs, t)
        put(n_refs, t + 1, many(left, get(n_refs, t)) + flag(t == inner) * eye)
        put(p_refs, t + 1, many(left, get(p_refs, t)))
        return carry

    lax.fori_loop(0, span - 1, chain, 0)
    across = many(get(a_refs, span - 1), get(p_refs, span - 1))
    bbuf[outer, 0] = pack(across[:BLK])
    bbuf[outer, 1] = pack(across[PAD : PAD + BLK])
    for t in reversed(outer_steps):
        hand(bbuf, (outer, core), t, b_send, b_recv, outer_peer(t))
    far, entering = across_spans(1, near, r_refs, m_refs, True)

    for t in outer_steps:
        origin = at_outer(-t)
        awaited(bbuf, (origin, core), t, b_send, b_recv)
        hand(bbuf, (origin, core), spans + t, b_send, b_recv, sibling)
    for t in outer_steps:
        awaited(bbuf, (at_outer(-t), 1 - core), spans + t, b_send, b_recv)
    lax.fori_loop(0, spans, functools.partial(unpack_all, bbuf), 0)
    mine_p = ph[inner].astype(F32) + pq[inner].astype(F32)
    mine_r = rh[inner].astype(F32) + rl[inner].astype(F32)
    put(m2_refs, spans - 1, jnp.zeros((RIM, RIM), F32))
    put(n2_refs, 0, jnp.zeros((RIM, RIM), F32))

    def outer_chain(t, carry):
        s = spans - 1 - t
        put(m2_refs, s - 1, many(get(m2_refs, s), get(a_refs, s)) + flag(s == outer) * mine_p)
        put(n2_refs, t + 1, many(get(a_refs, t), get(n2_refs, t)) + flag(t == outer) * mine_r)
        return carry

    lax.fori_loop(0, spans - 1, outer_chain, 0)

    solved, _ = forward_last(far, local, entering)
    direction, energy = backward(2, solved, place_system)
    answer = jnp.zeros_like(residual)
    for step in range(ITERS):
        phase = 4 * (step + 1)
        image = system_times(step, direction)
        near, local = forward_local(phase, image, lane_sum(direction * image))
        far, entering = across_spans(phase + 1, near, r_refs, m_refs, True)
        change, curvature = forward_last(far, local, entering)
        alpha = energy / curvature
        answer = answer + alpha * direction
        residual = residual - alpha * image
        solved = solved - alpha * change
        precond, energy_next = backward(phase + 2, solved)
        direction = precond + (energy_next / energy) * direction
        energy = energy_next

    for i in range(ROWS):
        lanes = slice(i * PAD, i * PAD + BLK)
        sol_ref[i] = answer[:, lanes]
        res_ref[i] = residual[:, lanes]
        dir_ref[i] = direction[:, lanes]
    for copy in sends:
        copy.wait_send()


def per_device(
    spans, cols, rhs, system_lower, system_diag, factor_lower, diag_inverse, neighbours, counts
):
    rows, width, columns = rhs.shape
    vmem = pl.BlockSpec(memory_space=pltpu.VMEM)
    phases = 4 * (ITERS + 1)
    half = lambda: pltpu.VMEM((GROUP, RIM, RIM), BF16)
    most = max(GROUP, spans)
    tall = lambda: pltpu.VMEM((most, RIM, RIM), BF16)
    dma = pltpu.SemaphoreType.DMA
    outs = pl.pallas_call(
        functools.partial(kernel, GROUP, spans, cols),
        out_shape=[jax.ShapeDtypeStruct((rows, columns, width), F32)] * 3,
        in_specs=[pl.BlockSpec(memory_space=pltpu.SMEM)] * 2 + [vmem] * 5,
        out_specs=[vmem] * 3,
        scratch_shapes=[
            pltpu.VMEM((WIDE, RIM + WIDE), F32),
            pltpu.VMEM((WIDE, RIM + WIDE), BF16),
            pltpu.VMEM((WIDE, RIM + WIDE), BF16),
            pltpu.VMEM((WIDE, RIM + WIDE), BF16),
            pltpu.VMEM((WIDE, RIM + WIDE), BF16),
            pltpu.VMEM((ROWS, PAD, PAD), BF16),
            pltpu.VMEM((ROWS, PAD, PAD), BF16),
            pltpu.VMEM((cols,) + system_lower.shape, F32),
            pltpu.VMEM((GROUP, 2, PACKED, PAD), F32),
            pltpu.VMEM((spans, 2, PACKED, PAD), F32),
            tall(), tall(),
            half(), half(), half(), half(), half(), half(), half(), half(),
            tall(), tall(), tall(), tall(),
            pltpu.VMEM((phases, most, columns, RIM), F32),
            pltpu.VMEM((ITERS, 2, columns, RIM), F32),
            pltpu.VMEM((ITERS, 2, columns, RIM), F32),
            dma, dma, dma((GROUP,)), dma((GROUP,)), dma((2 * spans,)), dma((2 * spans,)),
            dma((phases,)), dma((phases, most - 1)), dma((ITERS, 2)), dma((ITERS, 2)),
        ],
        compiler_params=pltpu.CompilerParams(
            collective_id=0, has_side_effects=True, vmem_limit_bytes=60 * 1024 * 1024
        ),
    )(
        neighbours, counts, jnp.transpose(rhs, (0, 2, 1)), system_lower, system_diag,
        factor_lower, diag_inverse,
    )
    return tuple(jnp.transpose(value, (0, 2, 1)) for value in outs)


def solution(mesh):
    in_specs = (
        P("row", None, "col"),
        P("row", "col", None, None),
        P("row", None, None),
        P("row", None, None, None),
        P("row", None, None),
        P("row", None),
        P("row"),
    )
    out_specs = (P("row", None, "col"), P("row", None, "col"), P("row", None, "col"))
    return jax.shard_map(
        functools.partial(per_device, mesh.shape["row"] // GROUP, mesh.shape["col"]),
        mesh=mesh, in_specs=in_specs, out_specs=out_specs, check_vma=False,
    )
```

time: 160 us -> 115 us (0.72)
  Pallas kernels: 151 us -> 110 us
  local copies, waits for them, and re-layouts: 6.13 us -> 4.42 us
    pallas_call x1, Pallas kernels: 151 us -> 110 us  [per_device(): pl.pallas_call(functools.partial(kernel, GROUP, spans, cols), out_shape=[...]
    unnamed x6 -> x3, local copies, waits for them, and re-layouts: 4.71 us -> 4.42 us
where the time goes in v2:
time: 115 us
  Pallas kernels  110 us (96%)
  local copies, waits for them, and re-layouts  4.42 us (4%)
    pallas_call x1, Pallas kernels, per_device(): pl.pallas_call(functools.partial(kernel, GROUP, spans, cols), out_shape=[...  110 us
    unnamed x3, local copies, waits for them, and re-layouts  4.42 us

profile of v2, /device:TPU:1, one launch (start us, length us, event | category | flops | bytes accessed | tf_op | source)
XLA Modules:
  0.0 114.7 jit_solution(6863244302708502096)
XLA Ops:
  0.6 109.6 %shard_map.94 = (f32[8,16,72]{2,1,0:T(8,128)}, f32[8,16,72]{2,1,0:T(8,128)}, f32[8,16,72]{2,1,0:T(8,128)}) custom-call(s32[8,8]{1,0:T(8,128)} %neighbours_ref.1, s32[8]{0:T(128)} %counts_ref.1, f32[8,16,72]{2,1,0:T(8,128)} %bitcast.4, f32[8,2,72,72]{3,2,1,0:T(8,128)} %sysl_ref.1, f32[8,72,72]{2,1,0:T(8,128)} %sysd_ref.1, f32[8,8,72,72]{3,2,1,0:T(8,128)} %fac_ref.1, ...), custom_call_target="tpu_custom_call" | custom-call | tf_op jit(solution)/shard_map/pallas_call | solution.py:448
  110.3 1.5 %copy.13 = f32[8,72,16]{1,2,0:T(8,128)} copy(f32[8,72,16]{1,2,0:T(8,128)} %bitcast.7) | data formatting | bytes 73728
  111.7 1.5 %copy.14 = f32[8,72,16]{1,2,0:T(8,128)} copy(f32[8,72,16]{1,2,0:T(8,128)} %bitcast.6) | data formatting | bytes 73728
  113.2 1.5 %copy.15 = f32[8,72,16]{1,2,0:T(8,128)} copy(f32[8,72,16]{1,2,0:T(8,128)} %bitcast.5) | data formatting | bytes 73728

commit v3 on v2

--- a/solution.py
+++ b/solution.py
@@ -75,10 +75,10 @@
 
 def kernel(
     span, spans, cols, neighbours_ref, counts_ref, rhs_ref, sysl_ref, sysd_ref, fac_ref, dinv_ref,
-    sol_ref, res_ref, dir_ref,
+    out_ref,
     dense, xh, xl, lh, ll, dh, dl, gathered, abuf, bbuf, ah, al,
     mh, ml, rh, rl, nh, nl, ph, pq, m2h, m2l, n2h, n2l, ex, nbs, nbr,
-    col_send, col_recv, a_send, a_recv, b_send, b_recv, ex_send, ex_recv, nb_send, nb_recv,
+    own_sem, col_send, col_recv, a_send, a_recv, b_send, b_recv, ex_send, ex_recv, nb_send, nb_recv,
 ):
     row, col = lax.axis_index("row"), lax.axis_index("col")
     total = span * spans
@@ -147,27 +147,41 @@
     dense[...] = jnp.zeros_like(dense)
     place(lambda i, k: fac_ref[i, k])
 
-    for i in range(ROWS):
-        inverse = padded(dinv_ref[i])
+    inverses = [padded(dinv_ref[i]) for i in range(ROWS)]
+    scaled = [
+        many(split(inverses[i]), split(dense[i * PAD : (i + 1) * PAD, : RIM + i * PAD]))
+        for i in range(ROWS)
+    ]
+    nothing = jnp.zeros((PAD, PAD), F32)
+    for i in range(0, ROWS, 2):
         width = RIM + i * PAD
-        given = dense[i * PAD : (i + 1) * PAD, :width]
-        scaled = many(split(inverse), split(given))
-        edge = scaled[:, :RIM]
+        first, second = scaled[i], scaled[i + 1][:, :width]
+        taken = many(
+            split(scaled[i + 1][:, width:]),
+            split(jnp.concatenate([first, inverses[i]], axis=1)),
+        )
+        rows = jnp.concatenate([first, second - taken[:, :width]], axis=0)
+        corner = jnp.concatenate(
+            [
+                jnp.concatenate([inverses[i], nothing], axis=1),
+                jnp.concatenate([-taken[:, width:], inverses[i + 1]], axis=1),
+            ],
+            axis=0,
+        )
+        edge = rows[:, :RIM]
         if i > 0:
-            step = many(
-                split(scaled[:, RIM:]), (xh[: i * PAD, :width], xl[: i * PAD, :width])
-            )
+            step = many(split(rows[:, RIM:]), (xh[: i * PAD, :width], xl[: i * PAD, :width]))
             edge = edge - step[:, :RIM]
-            body = [edge, -step[:, RIM:], inverse]
+            body = [edge, -step[:, RIM:], corner]
         else:
-            body = [edge, inverse]
-        if i < ROWS - 1:
-            body.append(jnp.zeros((PAD, WIDE - (i + 1) * PAD), F32))
+            body = [edge, corner]
+        if i < ROWS - 2:
+            body.append(jnp.zeros((2 * PAD, WIDE - (i + 2) * PAD), F32))
         high, low = split(jnp.concatenate(body, axis=1))
-        xh[i * PAD : (i + 1) * PAD, :] = high
-        xl[i * PAD : (i + 1) * PAD, :] = low
-        if i >= ROWS - 2:
-            abuf[inner, i - ROWS + 2] = pack(-edge[:BLK, :])
+        xh[i * PAD : (i + 2) * PAD, :] = high
+        xl[i * PAD : (i + 2) * PAD, :] = low
+    abuf[inner, 0] = pack(-edge[:BLK, :])
+    abuf[inner, 1] = pack(-edge[PAD : PAD + BLK, :])
 
     pl.semaphore_wait(barrier, len(greeted))
 
@@ -272,13 +286,10 @@
     def system_times(step, vector):
         vs = stacked(vector)
         falling = few(vs, lh[:, :RIM], ll[:, :RIM], False)
-        last = vector[:, tail:] + few(
-            vs[:, tail:], lh[tail:, RIM + tail :], ll[tail:, RIM + tail :], False
-        )
-        nbs[step, 0] = falling
-        nbs[step, 1] = last
         copies = []
-        for way, peer in ((0, down), (1, up)):
+
+        def pass_on(way, value, peer):
+            nbs[step, way] = value
             copy = remote(
                 nbs.at[step, way], nbr.at[step, way],
                 nb_send.at[step, way], nb_recv.at[step, way], peer,
@@ -286,6 +297,12 @@
             copy.start()
             copies.append(copy)
             sends.append(copy)
+
+        pass_on(0, falling, down)
+        last = vector[:, tail:] + few(
+            vs[:, tail:], lh[tail:, RIM + tail :], ll[tail:, RIM + tail :], False
+        )
+        pass_on(1, last, up)
         parts = []
         for i in range(3):
             a, b = i * RIM, (i + 1) * RIM
@@ -326,9 +343,11 @@
     others = gathered.at[pl.ds(0, cols - 1)]
     col_every = remote(others, others, col_send, col_recv, up)
     sends.append(col_every)
-    gathered[col] = sysl_ref[...]
+    own_copy = pltpu.make_async_copy(sysl_ref, gathered.at[col], own_sem)
+    own_copy.start()
 
     def place_system():
+        own_copy.wait()
         col_every.wait_recv()
         place(lambda i, k: gathered[k // share, i, k % share])
         for i in range(ROWS):
@@ -354,18 +373,31 @@
     def flag(condition):
         return jnp.where(condition, 1.0, 0.0).astype(F32)
 
-    def unpack_all(buf, s, carry):
+    def take_in(buf, s):
         put(a_refs, s, jnp.concatenate([unpack(buf[s, 0]), unpack(buf[s, 1])], axis=0))
-        return carry
-
+
+    take_in(abuf, inner)
+    awaited(abuf, at_inner(0, 1), 0, a_send, a_recv)
+    take_in(abuf, at_inner(0, 1))
     for x in nearest(chips):
         origin = at_inner(-x, 0)
         awaited(abuf, origin, x, a_send, a_recv)
         hand(abuf, origin, chips + x, a_send, a_recv, sibling)
-    awaited(abuf, at_inner(0, 1), 0, a_send, a_recv)
+        take_in(abuf, origin)
     for x in nearest(chips):
-        awaited(abuf, at_inner(-x, 1), chips + x, a_send, a_recv)
-    lax.fori_loop(0, span, functools.partial(unpack_all, abuf), 0)
+        origin = at_inner(-x, 1)
+        awaited(abuf, origin, chips + x, a_send, a_recv)
+        take_in(abuf, origin)
+
+    level = [get(a_refs, s) for s in range(span)]
+    while len(level) > 2:
+        level = [split(many(level[n + 1], level[n])) for n in range(0, len(level), 2)]
+    across = many(level[1], level[0])
+    bbuf[outer, 0] = pack(across[:BLK])
+    bbuf[outer, 1] = pack(across[PAD : PAD + BLK])
+    for t in reversed(outer_steps):
+        hand(bbuf, (outer, core), t, b_send, b_recv, outer_peer(t))
+
     put(m_refs, span - 1, jnp.zeros((RIM, RIM), F32))
     put(r_refs, span - 1, eye)
     put(n_refs, 0, jnp.zeros((RIM, RIM), F32))
@@ -382,20 +414,18 @@
         return carry
 
     lax.fori_loop(0, span - 1, chain, 0)
-    across = many(get(a_refs, span - 1), get(p_refs, span - 1))
-    bbuf[outer, 0] = pack(across[:BLK])
-    bbuf[outer, 1] = pack(across[PAD : PAD + BLK])
-    for t in reversed(outer_steps):
-        hand(bbuf, (outer, core), t, b_send, b_recv, outer_peer(t))
+
     far, entering = across_spans(1, near, r_refs, m_refs, True)
 
     for t in outer_steps:
         origin = at_outer(-t)
         awaited(bbuf, (origin, core), t, b_send, b_recv)
         hand(bbuf, (origin, core), spans + t, b_send, b_recv, sibling)
+    take_in(bbuf, outer)
     for t in outer_steps:
-        awaited(bbuf, (at_outer(-t), 1 - core), spans + t, b_send, b_recv)
-    lax.fori_loop(0, spans, functools.partial(unpack_all, bbuf), 0)
+        origin = at_outer(-t)
+        awaited(bbuf, (origin, 1 - core), spans + t, b_send, b_recv)
+        take_in(bbuf, origin)
     mine_p = ph[inner].astype(F32) + pq[inner].astype(F32)
     mine_r = rh[inner].astype(F32) + rl[inner].astype(F32)
     put(m2_refs, spans - 1, jnp.zeros((RIM, RIM), F32))
@@ -427,10 +457,10 @@
         energy = energy_next
 
     for i in range(ROWS):
-        lanes = slice(i * PAD, i * PAD + BLK)
-        sol_ref[i] = answer[:, lanes]
-        res_ref[i] = residual[:, lanes]
-        dir_ref[i] = direction[:, lanes]
+        lanes = slice(i * PAD, (i + 1) * PAD)
+        out_ref[0, i] = answer[:, lanes]
+        out_ref[1, i] = residual[:, lanes]
+        out_ref[2, i] = direction[:, lanes]
     for copy in sends:
         copy.wait_send()
 
@@ -447,9 +477,11 @@
     dma = pltpu.SemaphoreType.DMA
     outs = pl.pallas_call(
         functools.partial(kernel, GROUP, spans, cols),
-        out_shape=[jax.ShapeDtypeStruct((rows, columns, width), F32)] * 3,
-        in_specs=[pl.BlockSpec(memory_space=pltpu.SMEM)] * 2 + [vmem] * 5,
-        out_specs=[vmem] * 3,
+        out_shape=jax.ShapeDtypeStruct((3, rows, columns, PAD), F32),
+        in_specs=[pl.BlockSpec(memory_space=pltpu.SMEM)] * 2
+        + [vmem, pl.BlockSpec(memory_space=pl.ANY)]
+        + [vmem] * 3,
+        out_specs=vmem,
         scratch_shapes=[
             pltpu.VMEM((WIDE, RIM + WIDE), F32),
             pltpu.VMEM((WIDE, RIM + WIDE), BF16),
@@ -467,7 +499,7 @@
             pltpu.VMEM((phases, most, columns, RIM), F32),
             pltpu.VMEM((ITERS, 2, columns, RIM), F32),
             pltpu.VMEM((ITERS, 2, columns, RIM), F32),
-            dma, dma, dma((GROUP,)), dma((GROUP,)), dma((2 * spans,)), dma((2 * spans,)),
+            dma, dma, dma, dma((GROUP,)), dma((GROUP,)), dma((2 * spans,)), dma((2 * spans,)),
             dma((phases,)), dma((phases, most - 1)), dma((ITERS, 2)), dma((ITERS, 2)),
         ],
         compiler_params=pltpu.CompilerParams(
@@ -477,7 +509,7 @@
         neighbours, counts, jnp.transpose(rhs, (0, 2, 1)), system_lower, system_diag,
         factor_lower, diag_inverse,
     )
-    return tuple(jnp.transpose(value, (0, 2, 1)) for value in outs)
+    return tuple(jnp.transpose(outs[n, :, :, :width], (0, 2, 1)) for n in range(3))
 
 
 def solution(mesh):

time: 115 us -> 107 us (0.930)
  Pallas kernels: 110 us -> 104 us
  local copies, waits for them, and re-layouts: 4.42 us -> 1.58 us
    pallas_call x1, Pallas kernels: 110 us -> 104 us  [per_device(): pl.pallas_call(functools.partial(kernel, GROUP, spans, cols), out_shape=j...]
    unnamed x3 -> x0, local copies, waits for them, and re-layouts: 4.42 us -> none
    transpose x0 -> x1, local copies, waits for them, and re-layouts: none -> 1.58 us  [per_device(): jnp.transpose(outs[n, :, :, :width], (0, 2, 1))]
where the time goes in v3:
time: 107 us; the launch traced here: 106 us
  Pallas kernels  104 us (97%)
  local copies, waits for them, and re-layouts  1.58 us (1%)
    pallas_call x1, Pallas kernels, per_device(): pl.pallas_call(functools.partial(kernel, GROUP, spans, cols), out_shape=j...  104 us

profile of v3, /device:TPU:1, one launch (start us, length us, event | category | flops | bytes accessed | tf_op | source)
XLA Modules:
  0.0 106.5 jit_solution(8035155487455214021)
XLA Ops:
  0.6 104.3 %shard_map.94 = f32[3,8,16,128]{3,2,1,0:T(8,128)} custom-call(s32[8,8]{1,0:T(8,128)} %neighbours_ref.1, s32[8]{0:T(128)} %counts_ref.1, f32[8,16,72]{2,1,0:T(8,128)} %bitcast.13, f32[8,2,72,72]{3,2,1,0:T(8,128)} %sysl_ref.1, f32[8,72,72]{2,1,0:T(8,128)} %sysd_ref.1, f32[8,8,72,72]{3,2,1,0:T(8,128)} %fac_ref.1, f32[8,72,72]{2,1,0:T(8,128)} %dinv_ref.1), custom_call_target="tpu_custom_call" | custom-call | tf_op jit(solution)/shard_map/pallas_call | solution.py:478
  104.9 1.6 %slice_bitcast_fusion = (f32[8,72,16]{1,2,0:T(8,128)}, f32[8,72,16]{1,2,0:T(8,128)}, f32[8,72,16]{1,2,0:T(8,128)}) fusion(f32[3,8,16,128]{3,2,1,0:T(8,128)} %shard_map.94), kind=kLoop, calls=%fused_computation | loop fusion | bytes 221184 | tf_op jit(solution)/shard_map/transpose | solution.py:512

commit v4 on v3

--- a/solution.py
+++ b/solution.py
@@ -76,9 +76,9 @@
 def kernel(
     span, spans, cols, neighbours_ref, counts_ref, rhs_ref, sysl_ref, sysd_ref, fac_ref, dinv_ref,
     out_ref,
-    dense, xh, xl, lh, ll, dh, dl, gathered, abuf, bbuf, ah, al,
+    dense, xh, xl, lh, ll, dh, dl, gathered, abuf, bbuf, qbuf, ah, al, th, tl, wh, wl,
     mh, ml, rh, rl, nh, nl, ph, pq, m2h, m2l, n2h, n2l, ex, nbs, nbr,
-    own_sem, col_send, col_recv, a_send, a_recv, b_send, b_recv, ex_send, ex_recv, nb_send, nb_recv,
+    own_sem, col_send, col_recv, a_send, a_recv, b_send, b_recv, q_send, q_recv, ex_send, ex_recv, nb_send, nb_recv,
 ):
     row, col = lax.axis_index("row"), lax.axis_index("col")
     total = span * spans
@@ -193,9 +193,26 @@
     def awaited(buf, slot, n, send, recv):
         remote(buf.at[slot], buf.at[slot], send.at[n], recv.at[n], sibling).wait_recv()
 
-    for x in reversed(nearest(chips)):
-        hand(abuf, inner, x, a_send, a_recv, inner_peer(x, 0))
-    hand(abuf, inner, 0, a_send, a_recv, sibling)
+    def give(buf, send, recv):
+        for x in reversed(nearest(chips)):
+            hand(buf, inner, x, send, recv, inner_peer(x, 0))
+        hand(buf, inner, 0, send, recv, sibling)
+
+    def take(buf, send, recv, use):
+        use(inner)
+        awaited(buf, at_inner(0, 1), 0, send, recv)
+        use(at_inner(0, 1))
+        for x in nearest(chips):
+            origin = at_inner(-x, 0)
+            awaited(buf, origin, x, send, recv)
+            hand(buf, origin, chips + x, send, recv, sibling)
+            use(origin)
+        for x in nearest(chips):
+            origin = at_inner(-x, 1)
+            awaited(buf, origin, chips + x, send, recv)
+            use(origin)
+
+    give(abuf, a_send, a_recv)
 
     lane = lax.broadcasted_iota(jnp.int32, (columns, RIM), 1)
 
@@ -255,20 +272,30 @@
             parts.append(few(vs[:, :b], xh[a:b, RIM : RIM + b], xl[a:b, RIM : RIM + b], True))
         return near, jnp.concatenate(parts + [rim], axis=1)
 
-    def across_spans(phase, near, first, second, nt):
-        value, sums = collect(near, first, nt)
-        far = exchange(phase, with_sum(value, sums), 1)
-        return far, again(near, second, nt)
-
-    def forward_last(far, local, entering):
+    def forward_across(phase, near, local):
+        value, sums = collect(near, r_refs, True)
+        far = exchange(phase + 1, with_sum(value, sums), 1)
+        entering = again(near, m_refs, True)
+        local = local - few(stacked(entering), xh[:, :RIM], xl[:, :RIM], True)
+        rim = few(stacked(local), xh[:, :RIM], xl[:, :RIM], False)
+        return far, local, exchange(phase + 2, with_sum(rim, 0.0), 0)
+
+    def backward_inside(back):
+        value, _ = collect(back, p_refs, False)
+        return value, again(back, n_refs, False)
+
+    def forward_last(far, local, falling):
         value, sums = collect(far, m2_refs, True)
-        moved = few(stacked(entering + value), xh[:, :RIM], xl[:, :RIM], True)
-        return local - moved, sums
-
-    def backward(phase, source, beside=None):
+        vs = stacked(value)
+        local = local - few(vs, wh[...], wl[...], True)
+        spanned = falling[0] - few(vs, *get(t_refs, 0), False)
+        own = falling[1] - few(vs, *get(t_refs, 1), False)
+        return (local, spanned, own), sums
+
+    def backward(phase, state, beside=None):
+        source, spanned, own = state
+        far = exchange(phase + 3, with_sum(spanned, lane_sum(source * source)), 1)
         vs = stacked(source)
-        rim = few(vs, xh[:, :RIM], xl[:, :RIM], False)
-        near = exchange(phase, with_sum(rim, lane_sum(source * source)), 0)
         parts = []
         for i in range(4):
             a, b = i * RIM, (i + 1) * RIM
@@ -276,12 +303,19 @@
                 few(vs[:, a:], xh[a:, RIM + a : RIM + b], xl[a:, RIM + a : RIM + b], False)
             )
         local = jnp.concatenate(parts, axis=1)
-        far, entering = across_spans(phase + 1, near, p_refs, n_refs, False)
         if beside is not None:
             beside()
         value, sums = collect(far, n2_refs, False)
-        moved = few(stacked(entering + value), xh[tail:, RIM:], xl[tail:, RIM:], False)
-        return local - moved, sums
+        energy = exchange(phase + 4, jnp.where(lane == BLK, sums, 0.0), 0)
+        moved = few(stacked(own + value), xh[tail:, RIM:], xl[tail:, RIM:], False)
+        return local - moved, energy
+
+    def total_of(exchanged):
+        phase, _, value, coming = exchanged
+        for origin, copy in coming:
+            copy.wait_recv()
+            value = value + ex[phase, origin]
+        return lane_sum(jnp.where(lane == BLK, value, 0.0))
 
     def system_times(step, vector):
         vs = stacked(vector)
@@ -368,7 +402,7 @@
         refs[1][s] = low
 
     a_refs, m_refs, r_refs, n_refs, p_refs = (ah, al), (mh, ml), (rh, rl), (nh, nl), (ph, pq)
-    m2_refs, n2_refs = (m2h, m2l), (n2h, n2l)
+    m2_refs, n2_refs, t_refs = (m2h, m2l), (n2h, n2l), (th, tl)
 
     def flag(condition):
         return jnp.where(condition, 1.0, 0.0).astype(F32)
@@ -376,18 +410,12 @@
     def take_in(buf, s):
         put(a_refs, s, jnp.concatenate([unpack(buf[s, 0]), unpack(buf[s, 1])], axis=0))
 
-    take_in(abuf, inner)
-    awaited(abuf, at_inner(0, 1), 0, a_send, a_recv)
-    take_in(abuf, at_inner(0, 1))
-    for x in nearest(chips):
-        origin = at_inner(-x, 0)
-        awaited(abuf, origin, x, a_send, a_recv)
-        hand(abuf, origin, chips + x, a_send, a_recv, sibling)
-        take_in(abuf, origin)
-    for x in nearest(chips):
-        origin = at_inner(-x, 1)
-        awaited(abuf, origin, chips + x, a_send, a_recv)
-        take_in(abuf, origin)
+    edge = xh[:, :RIM].astype(F32) + xl[:, :RIM].astype(F32)
+    square = many(split(edge.T), (xh[:, :RIM], xl[:, :RIM]))
+    qbuf[inner, 0] = pack(square[:BLK])
+    qbuf[inner, 1] = pack(square[PAD : PAD + BLK])
+
+    take(abuf, a_send, a_recv, functools.partial(take_in, abuf))
 
     level = [get(a_refs, s) for s in range(span)]
     while len(level) > 2:
@@ -397,6 +425,8 @@
     bbuf[outer, 1] = pack(across[PAD : PAD + BLK])
     for t in reversed(outer_steps):
         hand(bbuf, (outer, core), t, b_send, b_recv, outer_peer(t))
+
+    give(qbuf, q_send, q_recv)
 
     put(m_refs, span - 1, jnp.zeros((RIM, RIM), F32))
     put(r_refs, span - 1, eye)
@@ -415,7 +445,23 @@
 
     lax.fori_loop(0, span - 1, chain, 0)
 
-    far, entering = across_spans(1, near, r_refs, m_refs, True)
+    far, local, back = forward_across(0, near, local)
+
+    entered = [jnp.zeros((RIM, RIM), F32), jnp.zeros((RIM, RIM), F32)]
+
+    def quadratic(s):
+        whole = jnp.concatenate([unpack(qbuf[s, 0]), unpack(qbuf[s, 1])], axis=0)
+        half = split(many(split(whole), get(p_refs, s)).T)
+        entered[0] += many(half, get(p_refs, s))
+        entered[1] += many(half, get(n_refs, s))
+
+    take(qbuf, q_send, q_recv, quadratic)
+    put(t_refs, 0, entered[0])
+    put(t_refs, 1, entered[1])
+    high, low = split(many((xh[:, :RIM], xl[:, :RIM]), get(p_refs, inner)))
+    wh[...] = high
+    wl[...] = low
+    falling = backward_inside(back)
 
     for t in outer_steps:
         origin = at_outer(-t)
@@ -426,34 +472,41 @@
         origin = at_outer(-t)
         awaited(bbuf, (origin, 1 - core), spans + t, b_send, b_recv)
         take_in(bbuf, origin)
-    mine_p = ph[inner].astype(F32) + pq[inner].astype(F32)
     mine_r = rh[inner].astype(F32) + rl[inner].astype(F32)
     put(m2_refs, spans - 1, jnp.zeros((RIM, RIM), F32))
     put(n2_refs, 0, jnp.zeros((RIM, RIM), F32))
 
     def outer_chain(t, carry):
         s = spans - 1 - t
-        put(m2_refs, s - 1, many(get(m2_refs, s), get(a_refs, s)) + flag(s == outer) * mine_p)
+        put(m2_refs, s - 1, many(get(m2_refs, s), get(a_refs, s)) + flag(s == outer) * eye)
         put(n2_refs, t + 1, many(get(a_refs, t), get(n2_refs, t)) + flag(t == outer) * mine_r)
         return carry
 
     lax.fori_loop(0, spans - 1, outer_chain, 0)
 
-    solved, _ = forward_last(far, local, entering)
-    direction, energy = backward(2, solved, place_system)
+    state, _ = forward_last(far, local, falling)
+    direction, waiting = backward(0, state, place_system)
+    image = system_times(0, direction)
+    energy = total_of(waiting)
     answer = jnp.zeros_like(residual)
     for step in range(ITERS):
-        phase = 4 * (step + 1)
-        image = system_times(step, direction)
+        phase = 5 * (step + 1)
         near, local = forward_local(phase, image, lane_sum(direction * image))
-        far, entering = across_spans(phase + 1, near, r_refs, m_refs, True)
-        change, curvature = forward_last(far, local, entering)
+        far, local, back = forward_across(phase, near, local)
+        falling = backward_inside(back)
+        change, curvature = forward_last(far, local, falling)
         alpha = energy / curvature
+        state = tuple(old - alpha * new for old, new in zip(state, change))
+        precond, waiting = backward(phase, state)
         answer = answer + alpha * direction
         residual = residual - alpha * image
-        solved = solved - alpha * change
-        precond, energy_next = backward(phase + 2, solved)
-        direction = precond + (energy_next / energy) * direction
+        if step < ITERS - 1:
+            following = system_times(step + 1, precond)
+        energy_next = total_of(waiting)
+        ratio = energy_next / energy
+        direction = precond + ratio * direction
+        if step < ITERS - 1:
+            image = following + ratio * image
         energy = energy_next
 
     for i in range(ROWS):
@@ -470,7 +523,7 @@
 ):
     rows, width, columns = rhs.shape
     vmem = pl.BlockSpec(memory_space=pltpu.VMEM)
-    phases = 4 * (ITERS + 1)
+    phases = 5 * (ITERS + 1)
     half = lambda: pltpu.VMEM((GROUP, RIM, RIM), BF16)
     most = max(GROUP, spans)
     tall = lambda: pltpu.VMEM((most, RIM, RIM), BF16)
@@ -493,13 +546,17 @@
             pltpu.VMEM((cols,) + system_lower.shape, F32),
             pltpu.VMEM((GROUP, 2, PACKED, PAD), F32),
             pltpu.VMEM((spans, 2, PACKED, PAD), F32),
+            pltpu.VMEM((GROUP, 2, PACKED, PAD), F32),
             tall(), tall(),
+            pltpu.VMEM((2, RIM, RIM), BF16), pltpu.VMEM((2, RIM, RIM), BF16),
+            pltpu.VMEM((WIDE, RIM), BF16), pltpu.VMEM((WIDE, RIM), BF16),
             half(), half(), half(), half(), half(), half(), half(), half(),
             tall(), tall(), tall(), tall(),
             pltpu.VMEM((phases, most, columns, RIM), F32),
             pltpu.VMEM((ITERS, 2, columns, RIM), F32),
             pltpu.VMEM((ITERS, 2, columns, RIM), F32),
             dma, dma, dma, dma((GROUP,)), dma((GROUP,)), dma((2 * spans,)), dma((2 * spans,)),
+            dma((GROUP,)), dma((GROUP,)),
             dma((phases,)), dma((phases, most - 1)), dma((ITERS, 2)), dma((ITERS, 2)),
         ],
         compiler_params=pltpu.CompilerParams(

time: 107 us -> 106 us (level)
  no operation moved by 1% of the time
where the time goes in v4:
time: 106 us
  Pallas kernels  104 us (98%)
  local copies, waits for them, and re-layouts  1.58 us (1%)
    pallas_call x1, Pallas kernels, per_device(): pl.pallas_call(functools.partial(kernel, GROUP, spans, cols), out_shape=j...  104 us

profile of v4, /device:TPU:1, one launch (start us, length us, event | category | flops | bytes accessed | tf_op | source)
XLA Modules:
  0.0 106.0 jit_solution(7537759869382414324)
XLA Ops:
  0.6 103.8 %shard_map.94 = f32[3,8,16,128]{3,2,1,0:T(8,128)} custom-call(s32[8,8]{1,0:T(8,128)} %neighbours_ref.1, s32[8]{0:T(128)} %counts_ref.1, f32[8,16,72]{2,1,0:T(8,128)} %bitcast.13, f32[8,2,72,72]{3,2,1,0:T(8,128)} %sysl_ref.1, f32[8,72,72]{2,1,0:T(8,128)} %sysd_ref.1, f32[8,8,72,72]{3,2,1,0:T(8,128)} %fac_ref.1, f32[8,72,72]{2,1,0:T(8,128)} %dinv_ref.1), custom_call_target="tpu_custom_call" | custom-call | tf_op jit(solution)/shard_map/pallas_call | solution.py:531
  104.5 1.6 %slice_bitcast_fusion = (f32[8,72,16]{1,2,0:T(8,128)}, f32[8,72,16]{1,2,0:T(8,128)}, f32[8,72,16]{1,2,0:T(8,128)}) fusion(f32[3,8,16,128]{3,2,1,0:T(8,128)} %shard_map.94), kind=kLoop, calls=%fused_computation | loop fusion | bytes 221184 | tf_op jit(solution)/shard_map/transpose | solution.py:569

commit v5 on v4

--- a/solution.py
+++ b/solution.py
@@ -251,7 +251,7 @@
             arrived = ex[phase, origin]
             value = value + arrived
             result += few(stacked(arrived), *get(refs, origin), nt)
-        return result, lane_sum(jnp.where(lane == BLK, value, 0.0))
+        return result, value
 
     def again(exchanged, refs, nt):
         phase, mine, value, coming = exchanged
@@ -272,17 +272,24 @@
             parts.append(few(vs[:, :b], xh[a:b, RIM : RIM + b], xl[a:b, RIM : RIM + b], True))
         return near, jnp.concatenate(parts + [rim], axis=1)
 
-    def forward_across(phase, near, local):
+    def pick(value, n):
+        return lane_sum(jnp.where(lane == BLK + n, value, 0.0))
+
+    def forward_across(phase, near, local, old=None):
         value, sums = collect(near, r_refs, True)
-        far = exchange(phase + 1, with_sum(value, sums), 1)
+        far = exchange(phase + 1, with_sum(value, pick(sums, 0)), 1)
         entering = again(near, m_refs, True)
         local = local - few(stacked(entering), xh[:, :RIM], xl[:, :RIM], True)
         rim = few(stacked(local), xh[:, :RIM], xl[:, :RIM], False)
-        return far, local, exchange(phase + 2, with_sum(rim, 0.0), 0)
+        value = with_sum(rim, 0.0)
+        if old is not None:
+            for n, (a, b) in enumerate(((old, old), (old, local), (local, local))):
+                value = jnp.where(lane == BLK + n, lane_sum(a * b), value)
+        return far, local, exchange(phase + 2, value, 0)
 
     def backward_inside(back):
-        value, _ = collect(back, p_refs, False)
-        return value, again(back, n_refs, False)
+        value, received = collect(back, p_refs, False)
+        return value, again(back, n_refs, False), received
 
     def forward_last(far, local, falling):
         value, sums = collect(far, m2_refs, True)
@@ -290,11 +297,12 @@
         local = local - few(vs, wh[...], wl[...], True)
         spanned = falling[0] - few(vs, *get(t_refs, 0), False)
         own = falling[1] - few(vs, *get(t_refs, 1), False)
-        return (local, spanned, own), sums
-
-    def backward(phase, state, beside=None):
+        return (local, spanned, own), pick(sums, 0), value
+
+    def backward(phase, state, beside=None, part=None):
         source, spanned, own = state
-        far = exchange(phase + 3, with_sum(spanned, lane_sum(source * source)), 1)
+        sums = lane_sum(source * source) if part is None else part
+        far = exchange(phase + 3, with_sum(spanned, sums), 1)
         vs = stacked(source)
         parts = []
         for i in range(4):
@@ -306,7 +314,9 @@
         if beside is not None:
             beside()
         value, sums = collect(far, n2_refs, False)
-        energy = exchange(phase + 4, jnp.where(lane == BLK, sums, 0.0), 0)
+        energy = pick(sums, 0)
+        if part is None:
+            energy = exchange(phase + 4, jnp.where(lane == BLK, energy, 0.0), 0)
         moved = few(stacked(own + value), xh[tail:, RIM:], xl[tail:, RIM:], False)
         return local - moved, energy
 
@@ -315,7 +325,7 @@
         for origin, copy in coming:
             copy.wait_recv()
             value = value + ex[phase, origin]
-        return lane_sum(jnp.where(lane == BLK, value, 0.0))
+        return pick(value, 0)
 
     def system_times(step, vector):
         vs = stacked(vector)
@@ -447,26 +457,25 @@
 
     far, local, back = forward_across(0, near, local)
 
-    entered = [jnp.zeros((RIM, RIM), F32), jnp.zeros((RIM, RIM), F32)]
-
-    def quadratic(s):
+    take(qbuf, q_send, q_recv, lambda s: None)
+    halves = []
+    for s in range(span):
         whole = jnp.concatenate([unpack(qbuf[s, 0]), unpack(qbuf[s, 1])], axis=0)
-        half = split(many(split(whole), get(p_refs, s)).T)
-        entered[0] += many(half, get(p_refs, s))
-        entered[1] += many(half, get(n_refs, s))
-
-    take(qbuf, q_send, q_recv, quadratic)
+        halves.append(split(many(split(whole), get(p_refs, s)).T))
+    entered = [
+        sum(many(halves[s], get(refs, s)) for s in range(span)) for refs in (p_refs, n_refs)
+    ]
     put(t_refs, 0, entered[0])
     put(t_refs, 1, entered[1])
     high, low = split(many((xh[:, :RIM], xl[:, :RIM]), get(p_refs, inner)))
     wh[...] = high
     wl[...] = low
-    falling = backward_inside(back)
 
     for t in outer_steps:
         origin = at_outer(-t)
         awaited(bbuf, (origin, core), t, b_send, b_recv)
         hand(bbuf, (origin, core), spans + t, b_send, b_recv, sibling)
+    falling = backward_inside(back)
     take_in(bbuf, outer)
     for t in outer_steps:
         origin = at_outer(-t)
@@ -484,7 +493,7 @@
 
     lax.fori_loop(0, spans - 1, outer_chain, 0)
 
-    state, _ = forward_last(far, local, falling)
+    state, _, _ = forward_last(far, local, falling)
     direction, waiting = backward(0, state, place_system)
     image = system_times(0, direction)
     energy = total_of(waiting)
@@ -492,20 +501,27 @@
     for step in range(ITERS):
         phase = 5 * (step + 1)
         near, local = forward_local(phase, image, lane_sum(direction * image))
-        far, local, back = forward_across(phase, near, local)
+        last = step == ITERS - 1
+        far, local, back = forward_across(phase, near, local, state[0] if last else None)
         falling = backward_inside(back)
-        change, curvature = forward_last(far, local, falling)
+        change, curvature, entering = forward_last(far, local, falling)
         alpha = energy / curvature
+        part = None
+        if last:
+            received = falling[2]
+            crossed = pick(received, 1) - lane_sum(state[1] * entering)
+            squared = pick(received, 2) - lane_sum((falling[0] + change[1]) * entering)
+            part = pick(received, 0) - alpha * (2.0 * crossed - alpha * squared)
         state = tuple(old - alpha * new for old, new in zip(state, change))
-        precond, waiting = backward(phase, state)
+        precond, waiting = backward(phase, state, part=part)
         answer = answer + alpha * direction
         residual = residual - alpha * image
-        if step < ITERS - 1:
+        if not last:
             following = system_times(step + 1, precond)
-        energy_next = total_of(waiting)
+        energy_next = waiting if last else total_of(waiting)
         ratio = energy_next / energy
         direction = precond + ratio * direction
-        if step < ITERS - 1:
+        if not last:
             image = following + ratio * image
         energy = energy_next
 
@@ -523,7 +539,7 @@
 ):
     rows, width, columns = rhs.shape
     vmem = pl.BlockSpec(memory_space=pltpu.VMEM)
-    phases = 5 * (ITERS + 1)
+    phases = 5 * (ITERS + 1) - 1
     half = lambda: pltpu.VMEM((GROUP, RIM, RIM), BF16)
     most = max(GROUP, spans)
     tall = lambda: pltpu.VMEM((most, RIM, RIM), BF16)

time: 106 us -> 100 us (0.943)
  Pallas kernels: 104 us -> 97.7 us
    pallas_call x1, Pallas kernels: 104 us -> 97.7 us  [per_device(): pl.pallas_call(functools.partial(kernel, GROUP, spans, cols), out_shape=j...]
where the time goes in v5:
time: 100 us; the launch traced here: 99.9 us
  Pallas kernels  97.7 us (98%)
  local copies, waits for them, and re-layouts  1.58 us (2%)
    pallas_call x1, Pallas kernels, per_device(): pl.pallas_call(functools.partial(kernel, GROUP, spans, cols), out_shape=j...  97.7 us

profile of v5, /device:TPU:1, one launch (start us, length us, event | category | flops | bytes accessed | tf_op | source)
XLA Modules:
  0.0 99.9 jit_solution(16426928242043497816)
XLA Ops:
  0.6 97.7 %shard_map.94 = f32[3,8,16,128]{3,2,1,0:T(8,128)} custom-call(s32[8,8]{1,0:T(8,128)} %neighbours_ref.1, s32[8]{0:T(128)} %counts_ref.1, f32[8,16,72]{2,1,0:T(8,128)} %bitcast.13, f32[8,2,72,72]{3,2,1,0:T(8,128)} %sysl_ref.1, f32[8,72,72]{2,1,0:T(8,128)} %sysd_ref.1, f32[8,8,72,72]{3,2,1,0:T(8,128)} %fac_ref.1, f32[8,72,72]{2,1,0:T(8,128)} %dinv_ref.1), custom_call_target="tpu_custom_call" | custom-call | tf_op jit(solution)/shard_map/pallas_call | solution.py:547
  98.3 1.6 %slice_bitcast_fusion = (f32[8,72,16]{1,2,0:T(8,128)}, f32[8,72,16]{1,2,0:T(8,128)}, f32[8,72,16]{1,2,0:T(8,128)}) fusion(f32[3,8,16,128]{3,2,1,0:T(8,128)} %shard_map.94), kind=kLoop, calls=%fused_computation | loop fusion | bytes 221184 | tf_op jit(solution)/shard_map/transpose | solution.py:585

commit v6 on v5

--- a/solution.py
+++ b/solution.py
@@ -491,13 +491,18 @@
         put(n2_refs, t + 1, many(get(a_refs, t), get(n2_refs, t)) + flag(t == outer) * mine_r)
         return carry
 
-    lax.fori_loop(0, spans - 1, outer_chain, 0)
+    lax.fori_loop(0, spans - 1, outer_chain, 0, unroll=True)
 
     state, _, _ = forward_last(far, local, falling)
     direction, waiting = backward(0, state, place_system)
     image = system_times(0, direction)
     energy = total_of(waiting)
     answer = jnp.zeros_like(residual)
+
+    def write(n, value):
+        for i in range(ROWS):
+            out_ref[n, i] = value[:, i * PAD : (i + 1) * PAD]
+
     for step in range(ITERS):
         phase = 5 * (step + 1)
         near, local = forward_local(phase, image, lane_sum(direction * image))
@@ -513,9 +518,20 @@
             squared = pick(received, 2) - lane_sum((falling[0] + change[1]) * entering)
             part = pick(received, 0) - alpha * (2.0 * crossed - alpha * squared)
         state = tuple(old - alpha * new for old, new in zip(state, change))
-        precond, waiting = backward(phase, state, part=part)
-        answer = answer + alpha * direction
-        residual = residual - alpha * image
+        held = []
+
+        def settle():
+            held.append(answer + alpha * direction)
+            held.append(residual - alpha * image)
+            if last:
+                write(0, held[0])
+                write(1, held[1])
+                for copy in sends[:-1]:
+                    copy.wait_send()
+                del sends[:-1]
+
+        precond, waiting = backward(phase, state, settle, part)
+        answer, residual = held
         if not last:
             following = system_times(step + 1, precond)
         energy_next = waiting if last else total_of(waiting)
@@ -525,11 +541,7 @@
             image = following + ratio * image
         energy = energy_next
 
-    for i in range(ROWS):
-        lanes = slice(i * PAD, (i + 1) * PAD)
-        out_ref[0, i] = answer[:, lanes]
-        out_ref[1, i] = residual[:, lanes]
-        out_ref[2, i] = direction[:, lanes]
+    write(2, direction)
     for copy in sends:
         copy.wait_send()
 

time: 100 us -> 99.5 us (level)
  no operation moved by 1% of the time
where the time goes in v6:
time: 99.5 us; the launch traced here: 99.1 us
  Pallas kernels  96.9 us (97%)
  local copies, waits for them, and re-layouts  1.58 us (2%)
    pallas_call x1, Pallas kernels, per_device(): pl.pallas_call(functools.partial(kernel, GROUP, spans, cols), out_shape=j...  96.9 us

profile of v6, /device:TPU:1, one launch (start us, length us, event | category | flops | bytes accessed | tf_op | source)
XLA Modules:
  0.0 99.1 jit_solution(1198640881786685215)
XLA Ops:
  0.6 96.9 %shard_map.94 = f32[3,8,16,128]{3,2,1,0:T(8,128)} custom-call(s32[8,8]{1,0:T(8,128)} %neighbours_ref.1, s32[8]{0:T(128)} %counts_ref.1, f32[8,16,72]{2,1,0:T(8,128)} %bitcast.13, f32[8,2,72,72]{3,2,1,0:T(8,128)} %sysl_ref.1, f32[8,72,72]{2,1,0:T(8,128)} %sysd_ref.1, f32[8,8,72,72]{3,2,1,0:T(8,128)} %fac_ref.1, f32[8,72,72]{2,1,0:T(8,128)} %dinv_ref.1), custom_call_target="tpu_custom_call" | custom-call | tf_op jit(solution)/shard_map/pallas_call | solution.py:559
  97.6 1.6 %slice_bitcast_fusion = (f32[8,72,16]{1,2,0:T(8,128)}, f32[8,72,16]{1,2,0:T(8,128)}, f32[8,72,16]{1,2,0:T(8,128)}) fusion(f32[3,8,16,128]{3,2,1,0:T(8,128)} %shard_map.94), kind=kLoop, calls=%fused_computation | loop fusion | bytes 221184 | tf_op jit(solution)/shard_map/transpose | solution.py:597

commit v7 on v6

--- a/solution.py
+++ b/solution.py
@@ -453,7 +453,7 @@
         put(p_refs, t + 1, many(left, get(p_refs, t)))
         return carry
 
-    lax.fori_loop(0, span - 1, chain, 0)
+    lax.fori_loop(0, span - 1, chain, 0, unroll=True)
 
     far, local, back = forward_across(0, near, local)
 

time: 99.5 us -> 99.1 us (level)
  no operation moved by 1% of the time
where the time goes in v7:
time: 99.1 us; the launch traced here: 99 us
  Pallas kernels  96.7 us (98%)
  local copies, waits for them, and re-layouts  1.58 us (2%)
    pallas_call x1, Pallas kernels, per_device(): pl.pallas_call(functools.partial(kernel, GROUP, spans, cols), out_shape=j...  96.7 us

profile of v7, /device:TPU:1, one launch (start us, length us, event | category | flops | bytes accessed | tf_op | source)
XLA Modules:
  0.0 99.0 jit_solution(10986444967957685411)
XLA Ops:
  0.6 96.7 %shard_map.94 = f32[3,8,16,128]{3,2,1,0:T(8,128)} custom-call(s32[8,8]{1,0:T(8,128)} %neighbours_ref.1, s32[8]{0:T(128)} %counts_ref.1, f32[8,16,72]{2,1,0:T(8,128)} %bitcast.13, f32[8,2,72,72]{3,2,1,0:T(8,128)} %sysl_ref.1, f32[8,72,72]{2,1,0:T(8,128)} %sysd_ref.1, f32[8,8,72,72]{3,2,1,0:T(8,128)} %fac_ref.1, f32[8,72,72]{2,1,0:T(8,128)} %dinv_ref.1), custom_call_target="tpu_custom_call" | custom-call | tf_op jit(solution)/shard_map/pallas_call | solution.py:559
  97.4 1.6 %slice_bitcast_fusion = (f32[8,72,16]{1,2,0:T(8,128)}, f32[8,72,16]{1,2,0:T(8,128)}, f32[8,72,16]{1,2,0:T(8,128)}) fusion(f32[3,8,16,128]{3,2,1,0:T(8,128)} %shard_map.94), kind=kLoop, calls=%fused_computation | loop fusion | bytes 221184 | tf_op jit(solution)/shard_map/transpose | solution.py:597
